TPU v7x, 32 devices: a whole 2x2x4 slice. The times are simulated.
32 devices in a mesh: ocean: 2 (over core), ice: 16 (over z, y, x).
Axes of the slice: x: 2, y: 2, z: 4, core: 2. Of those that a mesh axis runs over, the one named last changes fastest.
Arguments:
- velocity: float32 [128, 128, 128], P('ocean', 'ice'), may hold values from -6 to 6
- stress: float32 [128, 128, 128], P('ocean', 'ice'), may hold values from -6 to 6
- thickness: float32 [128, 128, 128], P('ocean', 'ice'), may hold values from 0.5 to 2
- forcing: float32 [128, 128, 128], P('ocean', 'ice'), may hold values from -6 to 6
- switch: int32 [128, 128, 128], P('ocean', 'ice'), may hold values 0 or 1
- covered: int32 [128], P('ocean'), may hold values from 0 to 1, as said below
- reinit: int32 [128], P('ocean'), may hold values 0 or 1
- cot_velocity: float32 [128, 128, 128], P('ocean', 'ice'), may hold values from -6 to 6
- cot_stress: float32 [128, 128, 128], P('ocean', 'ice'), may hold values from -6 to 6
- kernel: float32 [128, 128], replicated, may hold values from 0 to 1, as said below
Outputs:
- grad_velocity: float32 [128, 128, 128], P('ocean', 'ice')
- grad_stress: float32 [128, 128, 128], P('ocean', 'ice')
- grad_thickness: float32 [128, 128, 128], P('ocean', 'ice')
- grad_forcing: float32 [128, 128, 128], P('ocean', 'ice')
Inputs may be any that keep to these rules, and one draw needn't show every extreme that they name: Exactly 32 blocks are covered; one index of ocean holds 31 of them and the other holds one. The kernel's diagonal exceeds the sum of each row's other entries.
All inputs are finite; a program needn't handle non-finite values. No bound on the sum of `switch` or of `reinit` on one device may be relied on, other than what follows from the above.
Results may differ from a plain program's by a relative error of at most 0.00015.
Values sent between devices are 32-bit elements; how exact they have to be, the bound alone decides.
A program may use at most 64 MiB of HBM per device.

v0:
```python
import jax
import jax.numpy as jnp
from jax import lax
from jax.sharding import PartitionSpec as P

SUB = 8
WINDOWS = 2


PLASTIC = 0.25
VISCOUS = 1.0
GAMMA = 0.6
BETA = 0.9
STEP = 0.04


def passed_along(block, axis, distance):
    devices = range(lax.axis_size(axis))
    route = [(i - distance, i) for i in devices if i - distance in devices]
    return lax.ppermute(block, axis, route)


def prefix(part, axis, combine, identity):
    place = lax.axis_index(axis)
    gathered = lax.all_gather(part, axis)
    state = jnp.zeros_like(part) + jnp.asarray(identity, part.dtype)

    def one(turn, state):
        return combine(state, lax.dynamic_index_in_dim(gathered, turn, 0, False))

    return lax.fori_loop(0, place, one, state)


def forward_diff(x):
    above = passed_along(x[:, -1:], "ice", 1)
    upper = jnp.concatenate([above, x[:, :-1]], axis=1)
    left = jnp.pad(x, ((0, 0), (0, 0), (1, 0)))[:, :, :-1]
    return 2.0 * x - upper - left


def backward_diff(x):
    below = passed_along(x[:, :1], "ice", -1)
    lower = jnp.concatenate([x[:, 1:], below], axis=1)
    right = jnp.pad(x, ((0, 0), (0, 0), (0, 1)))[:, :, 1:]
    return 2.0 * x - lower - right


def ice_work(velo, stress_now, source, force, cot_u, cot_s, keep, kernel):
    rows_dev = velo.shape[1]
    first = lax.axis_index("ice") * rows_dev
    own_rows = lax.dynamic_slice_in_dim(kernel, first, rows_dev, 0)
    own_cols = lax.dynamic_slice_in_dim(kernel, first, rows_dev, 1)
    zeta = jnp.einsum(
        "ij,wjc->wic",
        own_rows,
        lax.all_gather(source, "ice", axis=1, tiled=True),
        precision=lax.Precision.HIGHEST,
    )
    scale = keep[:, None, None]

    def advance(carry, unused):
        u_now, s_now = carry
        strain = forward_diff(u_now)
        s_now = GAMMA * s_now + zeta * strain
        u_now = BETA * u_now - STEP * backward_diff(s_now) + STEP * force
        return ((u_now, s_now), strain)

    u_now, s_now = (velo, stress_now)
    strains = []
    for window in range(WINDOWS):
        if window > 0:
            s_now = s_now * scale
        (u_now, s_now), saved = lax.scan(advance, (u_now, s_now), None, length=SUB)
        strains.append(saved)

    def retreat(carry, strain):
        adj_u, adj_s, adj_z, adj_f = carry
        total_s = adj_s - STEP * forward_diff(adj_u)
        adj_f = adj_f + STEP * adj_u
        adj_u = BETA * adj_u + backward_diff(zeta * total_s)
        adj_z = adj_z + total_s * strain
        adj_s = GAMMA * total_s
        return ((adj_u, adj_s, adj_z, adj_f), None)

    zeros = jnp.zeros_like(velo)
    carry = (cot_u, cot_s, zeros, zeros)
    for window in range(WINDOWS - 1, -1, -1):
        carry, unused = lax.scan(retreat, carry, strains[window], reverse=True)
        if window > 0:
            carry = (carry[0], carry[1] * scale, carry[2], carry[3])
    adj_u, adj_s, adj_z, adj_f = carry
    adj_q = jnp.einsum(
        "ij,wic->wjc",
        own_cols,
        lax.all_gather(adj_z, "ice", axis=1, tiled=True),
        precision=lax.Precision.HIGHEST,
    )
    return (adj_u, adj_s, adj_q, adj_f)


def shards(
    velocity, stress, thickness, forcing, switch, covered, reinit, cot_velocity, cot_stress, kernel
):
    coef = jnp.where(switch == 1, PLASTIC, VISCOUS).astype(jnp.float32)
    source = thickness * coef
    keep = (1 - reinit).astype(jnp.float32)
    live = covered.astype(jnp.float32)[:, None, None]
    blocks = covered.shape[0]
    work = blocks // 4
    peers = lax.axis_size("ocean")
    cap = (min(blocks, work * peers) + peers - 1) // peers
    count = jnp.sum(covered)
    offset = prefix(count, "ocean", lambda early, late: early + late, jnp.int32(0))
    rank = jnp.cumsum(covered) - covered
    slot_ids = jnp.arange(peers * cap, dtype=jnp.int32)
    owner_of = slot_ids // cap
    place_of = slot_ids % cap
    wanted = place_of * peers + (owner_of - offset) % peers
    valid = wanted < count
    match = (covered[None, :] == 1) & (rank[None, :] == wanted[:, None])
    source_idx = jnp.sum(jnp.where(match, jnp.arange(blocks, dtype=jnp.int32)[None, :], 0), axis=1)
    work_slot = jnp.where(valid, (offset + wanted) // peers, -1).astype(jnp.float32)
    stacked = jnp.stack([velocity, stress, source, forcing, cot_velocity, cot_stress], axis=1)
    validf = valid.astype(jnp.float32)
    packed = jnp.take(stacked, source_idx, axis=0) * validf[:, None, None, None]
    keep_send = jnp.take(keep, source_idx, axis=0) * validf
    arrived, keep_recv, slot_recv = (
        lax.all_to_all(packed, "ocean", split_axis=0, concat_axis=0, tiled=True),
        lax.all_to_all(keep_send, "ocean", split_axis=0, concat_axis=0, tiled=True),
        lax.all_to_all(work_slot, "ocean", split_axis=0, concat_axis=0, tiled=True),
    )
    slot_int = slot_recv.astype(jnp.int32)
    picks = slot_int[None, :] == jnp.arange(work, dtype=jnp.int32)[:, None]
    pick_idx = jnp.sum(
        jnp.where(picks, jnp.arange(slot_int.shape[0], dtype=jnp.int32)[None, :], 0), axis=1
    )
    fields = jnp.take(arrived, pick_idx, axis=0)
    keep_work = jnp.take(keep_recv, pick_idx, axis=0)
    results = ice_work(
        fields[:, 0],
        fields[:, 1],
        fields[:, 2],
        fields[:, 3],
        fields[:, 4],
        fields[:, 5],
        keep_work,
        kernel,
    )
    gathered = jnp.stack(results, axis=1)
    present = (slot_int >= 0).astype(jnp.float32)
    outgoing = (
        jnp.take(gathered, jnp.clip(slot_int, 0, work - 1), axis=0) * present[:, None, None, None]
    )
    returned = lax.all_to_all(outgoing, "ocean", split_axis=0, concat_axis=0, tiled=True)
    global_idx = offset + rank
    home_slot = global_idx % peers * cap + rank // peers
    mine = jnp.take(returned, jnp.clip(home_slot, 0, peers * cap - 1), axis=0)
    grad_u, grad_s, grad_q, grad_f = (mine[:, 0], mine[:, 1], mine[:, 2], mine[:, 3])
    return (grad_u * live, grad_s * live, grad_q * coef * live, grad_f * live)


def solution(mesh):
    placed = (
        P("ocean", "ice", None),
        P("ocean", "ice", None),
        P("ocean", "ice", None),
        P("ocean", "ice", None),
        P("ocean", "ice", None),
        P("ocean"),
        P("ocean"),
        P("ocean", "ice", None),
        P("ocean", "ice", None),
        P(),
    )
    return jax.shard_map(
        shards,
        mesh=mesh,
        in_specs=placed,
        out_specs=(
            P("ocean", "ice", None),
            P("ocean", "ice", None),
            P("ocean", "ice", None),
            P("ocean", "ice", None),
        ),
        check_vma=False,
    )
```

profile of v0, /device:TPU:0, one launch (start us, length us, event | category | flops | bytes accessed | tf_op | source)
XLA Modules:
  0.0 590.0 jit_solution(14139794061866580057)
XLA Ops:
  38.3 58.4 %all-gather.6.cloned.1.call-done = f32[16,1,128,128]{3,2,0,1:T(8,128)} async-done(((f32[16,1,8,128]{3,2,0,1:T(8,128)}), f32[16,1,128,128]{3,2,0,1:T(8,128)}) %all-gather.6.cloned.1.call-update) | async-done | bytes 1048592 | tf_op jit(solution)/shard_map/all_gather | solution.py:56
  98.7 100.3 %while.84 = (s32[]{:T(128)}, f32[16,8,128]{2,1,0:T(8,128)S(1)}, f32[16,8,128]{2,1,0:T(8,128)S(1)}, f32[8,16,8,128]{3,2,1,0:T(8,128)S(1)}, f32[16,8,128]{2,1,0:T(...) while((s32[]{:T(128)}, f32[16,8,128]{2,1,0:T(8,128)S(1)}, f32[16,8,128]{2,1,0:T(8,128)S(1)}, ...), condition=%wide.region_7.8_spmd, body=%wide.region_6.7_spmd.sunk | while | flops 262146 | bytes 1073313 | solution.py:73
  104.0 4.5 collective-permute-done.1
  108.7 4.8 collective-permute-start
  116.3 4.5 collective-permute-done.1
  120.9 4.8 collective-permute-start
  128.5 4.5 collective-permute-done.1
  133.2 5.6 collective-permute-start
  141.6 4.5 collective-permute-done.1
  146.2 5.7 collective-permute-start
  154.8 4.5 collective-permute-done.1
  159.4 5.7 collective-permute-start
  167.9 4.5 collective-permute-done.1
  172.6 5.7 collective-permute-start
  181.1 4.5 collective-permute-done.1
  185.7 5.8 collective-permute-start
  194.3 4.5 collective-permute-done.1
  199.0 105.3 %while.85 = (s32[]{:T(128)}, f32[16,8,128]{2,1,0:T(8,128)S(1)}, f32[16,8,128]{2,1,0:T(8,128)S(1)}, f32[8,16,8,128]{3,2,1,0:T(8,128)S(1)}, f32[16,8,128]{2,1,0:T(...) while((s32[]{:T(128)}, f32[16,8,128]{2,1,0:T(8,128)S(1)}, f32[16,8,128]{2,1,0:T(8,128)S(1)}, ...), condition=%wide.region_9.10_spmd, body=%wide.region_8.9_spmd.sunk | while | flops 262146 | bytes 1073313 | solution.py:73
  199.1 5.7 collective-permute-start.2
  207.6 4.5 collective-permute-done.3
  212.3 5.7 collective-permute-start.2
  220.8 4.5 collective-permute-done.3
  225.4 5.7 collective-permute-start.2
  233.9 4.5 collective-permute-done.3
  238.6 5.7 collective-permute-start.2
  247.1 4.5 collective-permute-done.3
  251.7 5.7 collective-permute-start.2
  260.2 4.5 collective-permute-done.3
  264.9 5.7 collective-permute-start.2
  273.4 4.5 collective-permute-done.3
  278.0 5.7 collective-permute-start.2
  286.6 4.6 collective-permute-done.3
  291.3 5.7 collective-permute-start.2
  299.8 4.5 collective-permute-done.3
  304.4 105.2 %while.87 = (s32[]{:T(128)}, f32[16,8,128]{2,1,0:T(8,128)S(1)}, f32[16,8,128]{2,1,0:T(8,128)S(1)}, f32[16,8,128]{2,1,0:T(8,128)S(1)}, f32[16,8,128]{2,1,0:T(8,12...) while((s32[]{:T(128)}, f32[16,8,128]{2,1,0:T(8,128)S(1)}, ...), condition=%wide.region_11.12_spmd.clone, body=%wide.region_10.11_spmd.clone.sunk | while | flops 327684 | bytes 1327311 | solution.py:88
  304.4 5.7 collective-permute-start.6
  313.0 4.5 collective-permute-done.7
  317.6 5.7 collective-permute-start.6
  326.1 4.5 collective-permute-done.7
  330.7 5.7 collective-permute-start.6
  339.2 4.5 collective-permute-done.7
  343.9 5.7 collective-permute-start.6
  352.4 4.5 collective-permute-done.7
  357.0 5.7 collective-permute-start.6
  365.5 4.5 collective-permute-done.7
  370.2 5.7 collective-permute-start.6
  378.7 4.5 collective-permute-done.7
  383.3 5.7 collective-permute-start.6
  391.8 4.6 collective-permute-done.7
  396.5 5.6 collective-permute-start.6
  405.0 4.5 collective-permute-done.7
  409.7 105.2 %while.86 = (s32[]{:T(128)}, f32[16,8,128]{2,1,0:T(8,128)S(1)}, f32[16,8,128]{2,1,0:T(8,128)S(1)}, f32[16,8,128]{2,1,0:T(8,128)S(1)}, f32[16,8,128]{2,1,0:T(8,12...) while((s32[]{:T(128)}, f32[16,8,128]{2,1,0:T(8,128)S(1)}, ...), condition=%wide.region_13.14_spmd, body=%wide.region_12.13_spmd.sunk | while | flops 294915 | bytes 1327293 | solution.py:88
  409.7 5.7 collective-permute-start.4
  418.2 4.5 collective-permute-done.5
  422.8 5.7 collective-permute-start.4
  436.0 5.7 collective-permute-start.4
  449.1 5.7 collective-permute-start.4
  462.3 5.7 collective-permute-start.4
  475.4 5.7 collective-permute-start.4
  483.9 4.5 collective-permute-done.5
  488.6 5.7 collective-permute-start.4
  497.1 4.5 collective-permute-done.5
  501.7 5.7 collective-permute-start.4
  515.6 58.8 %all-gather.4.cloned.1.call-done = f32[16,128,128]{2,1,0:T(8,128)} async-done(((f32[16,8,128]{2,1,0:T(8,128)}), f32[16,128,128]{2,1,0:T(8,128)}) %all-gather.4.cloned.1.call-update) | async-done | bytes 1048592 | tf_op jit(solution)/shard_map/all_gather | solution.py:95
  (350 shorter events, 159.5 us)
Async XLA Ops:
  14.4 11.3 %all-to-all-start = ((f32[2,16,1]{1,2,0:T(1,128)}), f32[2,16,1]{1,2,0:T(1,128)S(1)}, u32[]{:S(2)}, u32[]{:S(2)}) async-start(f32[2,16,1]{1,2,0:T(1,128)} %bitcast.7), calls=%async_computation | async-start | bytes 2048 | tf_op jit(solution)/shard_map/all_to_all | solution.py:130
  34.9 61.8 %all-gather.6.cloned.1.call-start = ((), (), s32[]{:S(2)}) async-start(), calls=%async_computation.5 | async-start | bytes 1114112 | tf_op jit(solution)/shard_map/all_gather | solution.py:56
  38.3 536.2 %all-gather.4.cloned.1.call-start = ((), (), s32[]{:S(2)}) async-start(), calls=%async_computation.4 | async-start | bytes 1114112 | tf_op jit(solution)/shard_map/all_gather | solution.py:95
  102.7 5.8 collective-permute-start.1
  108.7 6.2 %collective-permute-start = (f32[16,1,128]{2,1,0:T(1,128)S(1)}, f32[16,1,128]{2,1,0:T(1,128)S(1)}, u32[]{:S(2)}, u32[]{:S(2)}) collective-permute-start(f32[16,1,128]{2,1,0:T(1,128)S(1)} %slice.343), channel_id=1, source_target_pairs={{0,1},{1,2},{2,3},{3,4},{4,5},{5,6},{6,7},{7,8},{8,9},{9,10},{10,1... | collective-permute-start | bytes 24584 | tf_op jit(solution)/shard_map/while/body/eval_jaxpr/ppermute | solution.py:20
  115.0 5.8 collective-permute-start.1
  120.9 6.2 %collective-permute-start = (f32[16,1,128]{2,1,0:T(1,128)S(1)}, f32[16,1,128]{2,1,0:T(1,128)S(1)}, u32[]{:S(2)}, u32[]{:S(2)}) collective-permute-start(f32[16,1,128]{2,1,0:T(1,128)S(1)} %slice.343), channel_id=1, source_target_pairs={{0,1},{1,2},{2,3},{3,4},{4,5},{5,6},{6,7},{7,8},{8,9},{9,10},{10,1... | collective-permute-start | bytes 24584 | tf_op jit(solution)/shard_map/while/body/eval_jaxpr/ppermute | solution.py:20
  127.2 5.8 collective-permute-start.1
  133.2 7.0 %collective-permute-start = (f32[16,1,128]{2,1,0:T(1,128)S(1)}, f32[16,1,128]{2,1,0:T(1,128)S(1)}, u32[]{:S(2)}, u32[]{:S(2)}) collective-permute-start(f32[16,1,128]{2,1,0:T(1,128)S(1)} %slice.343), channel_id=1, source_target_pairs={{0,1},{1,2},{2,3},{3,4},{4,5},{5,6},{6,7},{7,8},{8,9},{9,10},{10,1... | collective-permute-start | bytes 24584 | tf_op jit(solution)/shard_map/while/body/eval_jaxpr/ppermute | solution.py:20
  140.3 5.8 collective-permute-start.1
  146.2 7.1 %collective-permute-start = (f32[16,1,128]{2,1,0:T(1,128)S(1)}, f32[16,1,128]{2,1,0:T(1,128)S(1)}, u32[]{:S(2)}, u32[]{:S(2)}) collective-permute-start(f32[16,1,128]{2,1,0:T(1,128)S(1)} %slice.343), channel_id=1, source_target_pairs={{0,1},{1,2},{2,3},{3,4},{4,5},{5,6},{6,7},{7,8},{8,9},{9,10},{10,1... | collective-permute-start | bytes 24584 | tf_op jit(solution)/shard_map/while/body/eval_jaxpr/ppermute | solution.py:20
  153.5 5.8 collective-permute-start.1
  159.4 7.1 %collective-permute-start = (f32[16,1,128]{2,1,0:T(1,128)S(1)}, f32[16,1,128]{2,1,0:T(1,128)S(1)}, u32[]{:S(2)}, u32[]{:S(2)}) collective-permute-start(f32[16,1,128]{2,1,0:T(1,128)S(1)} %slice.343), channel_id=1, source_target_pairs={{0,1},{1,2},{2,3},{3,4},{4,5},{5,6},{6,7},{7,8},{8,9},{9,10},{10,1... | collective-permute-start | bytes 24584 | tf_op jit(solution)/shard_map/while/body/eval_jaxpr/ppermute | solution.py:20
  166.6 5.8 collective-permute-start.1
  172.6 7.1 %collective-permute-start = (f32[16,1,128]{2,1,0:T(1,128)S(1)}, f32[16,1,128]{2,1,0:T(1,128)S(1)}, u32[]{:S(2)}, u32[]{:S(2)}) collective-permute-start(f32[16,1,128]{2,1,0:T(1,128)S(1)} %slice.343), channel_id=1, source_target_pairs={{0,1},{1,2},{2,3},{3,4},{4,5},{5,6},{6,7},{7,8},{8,9},{9,10},{10,1... | collective-permute-start | bytes 24584 | tf_op jit(solution)/shard_map/while/body/eval_jaxpr/ppermute | solution.py:20
  179.8 5.8 collective-permute-start.1
  185.7 7.1 %collective-permute-start = (f32[16,1,128]{2,1,0:T(1,128)S(1)}, f32[16,1,128]{2,1,0:T(1,128)S(1)}, u32[]{:S(2)}, u32[]{:S(2)}) collective-permute-start(f32[16,1,128]{2,1,0:T(1,128)S(1)} %slice.343), channel_id=1, source_target_pairs={{0,1},{1,2},{2,3},{3,4},{4,5},{5,6},{6,7},{7,8},{8,9},{9,10},{10,1... | collective-permute-start | bytes 24584 | tf_op jit(solution)/shard_map/while/body/eval_jaxpr/ppermute | solution.py:20
  193.0 5.8 collective-permute-start.1
  199.1 7.1 %collective-permute-start.2 = (f32[16,1,128]{2,1,0:T(1,128)S(1)}, f32[16,1,128]{2,1,0:T(1,128)S(1)}, u32[]{:S(2)}, u32[]{:S(2)}) collective-permute-start(f32[16,1,128]{2,1,0:T(1,128)S(1)} %slice.347), channel_id=1, source_target_pairs={{0,1},{1,2},{2,3},{3,4},{4,5},{5,6},{6,7},{7,8},{8,9},{9,10},{10,1... | collective-permute-start | bytes 24584 | tf_op jit(solution)/shard_map/while/body/eval_jaxpr/ppermute | solution.py:20
  206.3 5.9 collective-permute-start.3
  212.3 7.0 %collective-permute-start.2 = (f32[16,1,128]{2,1,0:T(1,128)S(1)}, f32[16,1,128]{2,1,0:T(1,128)S(1)}, u32[]{:S(2)}, u32[]{:S(2)}) collective-permute-start(f32[16,1,128]{2,1,0:T(1,128)S(1)} %slice.347), channel_id=1, source_target_pairs={{0,1},{1,2},{2,3},{3,4},{4,5},{5,6},{6,7},{7,8},{8,9},{9,10},{10,1... | collective-permute-start | bytes 24584 | tf_op jit(solution)/shard_map/while/body/eval_jaxpr/ppermute | solution.py:20
  219.4 5.8 collective-permute-start.3
  225.4 7.1 %collective-permute-start.2 = (f32[16,1,128]{2,1,0:T(1,128)S(1)}, f32[16,1,128]{2,1,0:T(1,128)S(1)}, u32[]{:S(2)}, u32[]{:S(2)}) collective-permute-start(f32[16,1,128]{2,1,0:T(1,128)S(1)} %slice.347), channel_id=1, source_target_pairs={{0,1},{1,2},{2,3},{3,4},{4,5},{5,6},{6,7},{7,8},{8,9},{9,10},{10,1... | collective-permute-start | bytes 24584 | tf_op jit(solution)/shard_map/while/body/eval_jaxpr/ppermute | solution.py:20
  232.6 5.8 collective-permute-start.3
  238.6 7.1 %collective-permute-start.2 = (f32[16,1,128]{2,1,0:T(1,128)S(1)}, f32[16,1,128]{2,1,0:T(1,128)S(1)}, u32[]{:S(2)}, u32[]{:S(2)}) collective-permute-start(f32[16,1,128]{2,1,0:T(1,128)S(1)} %slice.347), channel_id=1, source_target_pairs={{0,1},{1,2},{2,3},{3,4},{4,5},{5,6},{6,7},{7,8},{8,9},{9,10},{10,1... | collective-permute-start | bytes 24584 | tf_op jit(solution)/shard_map/while/body/eval_jaxpr/ppermute | solution.py:20
  245.8 5.8 collective-permute-start.3
  251.7 7.1 %collective-permute-start.2 = (f32[16,1,128]{2,1,0:T(1,128)S(1)}, f32[16,1,128]{2,1,0:T(1,128)S(1)}, u32[]{:S(2)}, u32[]{:S(2)}) collective-permute-start(f32[16,1,128]{2,1,0:T(1,128)S(1)} %slice.347), channel_id=1, source_target_pairs={{0,1},{1,2},{2,3},{3,4},{4,5},{5,6},{6,7},{7,8},{8,9},{9,10},{10,1... | collective-permute-start | bytes 24584 | tf_op jit(solution)/shard_map/while/body/eval_jaxpr/ppermute | solution.py:20
  258.9 5.8 collective-permute-start.3
  264.9 7.1 %collective-permute-start.2 = (f32[16,1,128]{2,1,0:T(1,128)S(1)}, f32[16,1,128]{2,1,0:T(1,128)S(1)}, u32[]{:S(2)}, u32[]{:S(2)}) collective-permute-start(f32[16,1,128]{2,1,0:T(1,128)S(1)} %slice.347), channel_id=1, source_target_pairs={{0,1},{1,2},{2,3},{3,4},{4,5},{5,6},{6,7},{7,8},{8,9},{9,10},{10,1... | collective-permute-start | bytes 24584 | tf_op jit(solution)/shard_map/while/body/eval_jaxpr/ppermute | solution.py:20
  272.1 5.8 collective-permute-start.3
  278.0 7.1 %collective-permute-start.2 = (f32[16,1,128]{2,1,0:T(1,128)S(1)}, f32[16,1,128]{2,1,0:T(1,128)S(1)}, u32[]{:S(2)}, u32[]{:S(2)}) collective-permute-start(f32[16,1,128]{2,1,0:T(1,128)S(1)} %slice.347), channel_id=1, source_target_pairs={{0,1},{1,2},{2,3},{3,4},{4,5},{5,6},{6,7},{7,8},{8,9},{9,10},{10,1... | collective-permute-start | bytes 24584 | tf_op jit(solution)/shard_map/while/body/eval_jaxpr/ppermute | solution.py:20
  285.2 5.9 collective-permute-start.3
  291.3 7.1 %collective-permute-start.2 = (f32[16,1,128]{2,1,0:T(1,128)S(1)}, f32[16,1,128]{2,1,0:T(1,128)S(1)}, u32[]{:S(2)}, u32[]{:S(2)}) collective-permute-start(f32[16,1,128]{2,1,0:T(1,128)S(1)} %slice.347), channel_id=1, source_target_pairs={{0,1},{1,2},{2,3},{3,4},{4,5},{5,6},{6,7},{7,8},{8,9},{9,10},{10,1... | collective-permute-start | bytes 24584 | tf_op jit(solution)/shard_map/while/body/eval_jaxpr/ppermute | solution.py:20
  298.5 5.8 collective-permute-start.3
  304.4 7.1 %collective-permute-start.6 = (f32[16,1,128]{2,1,0:T(1,128)S(1)}, f32[16,1,128]{2,1,0:T(1,128)S(1)}, u32[]{:S(2)}, u32[]{:S(2)}) collective-permute-start(f32[16,1,128]{2,1,0:T(1,128)S(1)} %slice.355), channel_id=1, source_target_pairs={{0,1},{1,2},{2,3},{3,4},{4,5},{5,6},{6,7},{7,8},{8,9},{9,10},{10,1... | collective-permute-start | bytes 24584 | tf_op jit(solution)/shard_map/while/body/eval_jaxpr/ppermute | solution.py:20
  311.6 5.8 collective-permute-start.7
  317.6 7.1 %collective-permute-start.6 = (f32[16,1,128]{2,1,0:T(1,128)S(1)}, f32[16,1,128]{2,1,0:T(1,128)S(1)}, u32[]{:S(2)}, u32[]{:S(2)}) collective-permute-start(f32[16,1,128]{2,1,0:T(1,128)S(1)} %slice.355), channel_id=1, source_target_pairs={{0,1},{1,2},{2,3},{3,4},{4,5},{5,6},{6,7},{7,8},{8,9},{9,10},{10,1... | collective-permute-start | bytes 24584 | tf_op jit(solution)/shard_map/while/body/eval_jaxpr/ppermute | solution.py:20
  324.8 5.8 collective-permute-start.7
  330.7 7.1 %collective-permute-start.6 = (f32[16,1,128]{2,1,0:T(1,128)S(1)}, f32[16,1,128]{2,1,0:T(1,128)S(1)}, u32[]{:S(2)}, u32[]{:S(2)}) collective-permute-start(f32[16,1,128]{2,1,0:T(1,128)S(1)} %slice.355), channel_id=1, source_target_pairs={{0,1},{1,2},{2,3},{3,4},{4,5},{5,6},{6,7},{7,8},{8,9},{9,10},{10,1... | collective-permute-start | bytes 24584 | tf_op jit(solution)/shard_map/while/body/eval_jaxpr/ppermute | solution.py:20
  337.9 5.8 collective-permute-start.7
  343.9 7.1 %collective-permute-start.6 = (f32[16,1,128]{2,1,0:T(1,128)S(1)}, f32[16,1,128]{2,1,0:T(1,128)S(1)}, u32[]{:S(2)}, u32[]{:S(2)}) collective-permute-start(f32[16,1,128]{2,1,0:T(1,128)S(1)} %slice.355), channel_id=1, source_target_pairs={{0,1},{1,2},{2,3},{3,4},{4,5},{5,6},{6,7},{7,8},{8,9},{9,10},{10,1... | collective-permute-start | bytes 24584 | tf_op jit(solution)/shard_map/while/body/eval_jaxpr/ppermute | solution.py:20
  351.1 5.8 collective-permute-start.7
  357.0 7.1 %collective-permute-start.6 = (f32[16,1,128]{2,1,0:T(1,128)S(1)}, f32[16,1,128]{2,1,0:T(1,128)S(1)}, u32[]{:S(2)}, u32[]{:S(2)}) collective-permute-start(f32[16,1,128]{2,1,0:T(1,128)S(1)} %slice.355), channel_id=1, source_target_pairs={{0,1},{1,2},{2,3},{3,4},{4,5},{5,6},{6,7},{7,8},{8,9},{9,10},{10,1... | collective-permute-start | bytes 24584 | tf_op jit(solution)/shard_map/while/body/eval_jaxpr/ppermute | solution.py:20
  364.2 5.8 collective-permute-start.7
  370.2 7.1 %collective-permute-start.6 = (f32[16,1,128]{2,1,0:T(1,128)S(1)}, f32[16,1,128]{2,1,0:T(1,128)S(1)}, u32[]{:S(2)}, u32[]{:S(2)}) collective-permute-start(f32[16,1,128]{2,1,0:T(1,128)S(1)} %slice.355), channel_id=1, source_target_pairs={{0,1},{1,2},{2,3},{3,4},{4,5},{5,6},{6,7},{7,8},{8,9},{9,10},{10,1... | collective-permute-start | bytes 24584 | tf_op jit(solution)/shard_map/while/body/eval_jaxpr/ppermute | solution.py:20
  377.4 5.8 collective-permute-start.7
  383.3 7.1 %collective-permute-start.6 = (f32[16,1,128]{2,1,0:T(1,128)S(1)}, f32[16,1,128]{2,1,0:T(1,128)S(1)}, u32[]{:S(2)}, u32[]{:S(2)}) collective-permute-start(f32[16,1,128]{2,1,0:T(1,128)S(1)} %slice.355), channel_id=1, source_target_pairs={{0,1},{1,2},{2,3},{3,4},{4,5},{5,6},{6,7},{7,8},{8,9},{9,10},{10,1... | collective-permute-start | bytes 24584 | tf_op jit(solution)/shard_map/while/body/eval_jaxpr/ppermute | solution.py:20
  390.5 5.9 collective-permute-start.7
  396.5 7.0 %collective-permute-start.6 = (f32[16,1,128]{2,1,0:T(1,128)S(1)}, f32[16,1,128]{2,1,0:T(1,128)S(1)}, u32[]{:S(2)}, u32[]{:S(2)}) collective-permute-start(f32[16,1,128]{2,1,0:T(1,128)S(1)} %slice.355), channel_id=1, source_target_pairs={{0,1},{1,2},{2,3},{3,4},{4,5},{5,6},{6,7},{7,8},{8,9},{9,10},{10,1... | collective-permute-start | bytes 24584 | tf_op jit(solution)/shard_map/while/body/eval_jaxpr/ppermute | solution.py:20
  403.7 5.8 collective-permute-start.7
  409.7 7.1 %collective-permute-start.4 = (f32[16,1,128]{2,1,0:T(1,128)S(1)}, f32[16,1,128]{2,1,0:T(1,128)S(1)}, u32[]{:S(2)}, u32[]{:S(2)}) collective-permute-start(f32[16,1,128]{2,1,0:T(1,128)S(1)} %slice.351), channel_id=1, source_target_pairs={{0,1},{1,2},{2,3},{3,4},{4,5},{5,6},{6,7},{7,8},{8,9},{9,10},{10,1... | collective-permute-start | bytes 24584 | tf_op jit(solution)/shard_map/while/body/eval_jaxpr/ppermute | solution.py:20
  416.9 5.8 collective-permute-start.5
  422.8 7.1 %collective-permute-start.4 = (f32[16,1,128]{2,1,0:T(1,128)S(1)}, f32[16,1,128]{2,1,0:T(1,128)S(1)}, u32[]{:S(2)}, u32[]{:S(2)}) collective-permute-start(f32[16,1,128]{2,1,0:T(1,128)S(1)} %slice.351), channel_id=1, source_target_pairs={{0,1},{1,2},{2,3},{3,4},{4,5},{5,6},{6,7},{7,8},{8,9},{9,10},{10,1... | collective-permute-start | bytes 24584 | tf_op jit(solution)/shard_map/while/body/eval_jaxpr/ppermute | solution.py:20
  430.0 5.8 collective-permute-start.5
  436.0 7.1 %collective-permute-start.4 = (f32[16,1,128]{2,1,0:T(1,128)S(1)}, f32[16,1,128]{2,1,0:T(1,128)S(1)}, u32[]{:S(2)}, u32[]{:S(2)}) collective-permute-start(f32[16,1,128]{2,1,0:T(1,128)S(1)} %slice.351), channel_id=1, source_target_pairs={{0,1},{1,2},{2,3},{3,4},{4,5},{5,6},{6,7},{7,8},{8,9},{9,10},{10,1... | collective-permute-start | bytes 24584 | tf_op jit(solution)/shard_map/while/body/eval_jaxpr/ppermute | solution.py:20
  443.2 5.8 collective-permute-start.5
  449.1 7.1 %collective-permute-start.4 = (f32[16,1,128]{2,1,0:T(1,128)S(1)}, f32[16,1,128]{2,1,0:T(1,128)S(1)}, u32[]{:S(2)}, u32[]{:S(2)}) collective-permute-start(f32[16,1,128]{2,1,0:T(1,128)S(1)} %slice.351), channel_id=1, source_target_pairs={{0,1},{1,2},{2,3},{3,4},{4,5},{5,6},{6,7},{7,8},{8,9},{9,10},{10,1... | collective-permute-start | bytes 24584 | tf_op jit(solution)/shard_map/while/body/eval_jaxpr/ppermute | solution.py:20
  456.3 5.8 collective-permute-start.5
  462.3 7.1 %collective-permute-start.4 = (f32[16,1,128]{2,1,0:T(1,128)S(1)}, f32[16,1,128]{2,1,0:T(1,128)S(1)}, u32[]{:S(2)}, u32[]{:S(2)}) collective-permute-start(f32[16,1,128]{2,1,0:T(1,128)S(1)} %slice.351), channel_id=1, source_target_pairs={{0,1},{1,2},{2,3},{3,4},{4,5},{5,6},{6,7},{7,8},{8,9},{9,10},{10,1... | collective-permute-start | bytes 24584 | tf_op jit(solution)/shard_map/while/body/eval_jaxpr/ppermute | solution.py:20
  469.5 5.8 collective-permute-start.5
  475.4 7.1 %collective-permute-start.4 = (f32[16,1,128]{2,1,0:T(1,128)S(1)}, f32[16,1,128]{2,1,0:T(1,128)S(1)}, u32[]{:S(2)}, u32[]{:S(2)}) collective-permute-start(f32[16,1,128]{2,1,0:T(1,128)S(1)} %slice.351), channel_id=1, source_target_pairs={{0,1},{1,2},{2,3},{3,4},{4,5},{5,6},{6,7},{7,8},{8,9},{9,10},{10,1... | collective-permute-start | bytes 24584 | tf_op jit(solution)/shard_map/while/body/eval_jaxpr/ppermute | solution.py:20
  488.6 7.1 %collective-permute-start.4 = (f32[16,1,128]{2,1,0:T(1,128)S(1)}, f32[16,1,128]{2,1,0:T(1,128)S(1)}, u32[]{:S(2)}, u32[]{:S(2)}) collective-permute-start(f32[16,1,128]{2,1,0:T(1,128)S(1)} %slice.351), channel_id=1, source_target_pairs={{0,1},{1,2},{2,3},{3,4},{4,5},{5,6},{6,7},{7,8},{8,9},{9,10},{10,1... | collective-permute-start | bytes 24584 | tf_op jit(solution)/shard_map/while/body/eval_jaxpr/ppermute | solution.py:20
  495.8 5.8 collective-permute-start.5
  501.7 7.1 %collective-permute-start.4 = (f32[16,1,128]{2,1,0:T(1,128)S(1)}, f32[16,1,128]{2,1,0:T(1,128)S(1)}, u32[]{:S(2)}, u32[]{:S(2)}) collective-permute-start(f32[16,1,128]{2,1,0:T(1,128)S(1)} %slice.351), channel_id=1, source_target_pairs={{0,1},{1,2},{2,3},{3,4},{4,5},{5,6},{6,7},{7,8},{8,9},{9,10},{10,1... | collective-permute-start | bytes 24584 | tf_op jit(solution)/shard_map/while/body/eval_jaxpr/ppermute | solution.py:20
  (12 other events, 189.5 us)
Sparse Core Ops, SparseCore 0:
  39.0 57.6 all-gather.5
  515.6 58.7 all-gather.3
where the time goes:
time: 593 us; the launch traced here: 590 us
  waiting for transfers between devices  306 us (52%)
  starting transfers between devices  229 us (39%)
  other arithmetic  16.6 us (3%)
  between operations  14.4 us (2%)
  local copies, waits for them, and re-layouts  12.3 us (2%)
  blocking collectives  6.08 us (1%)
    ppermute x64, starting transfers between devices, passed_along(): return lax.ppermute(block, axis, route)  219 us
    ppermute x64, waiting for transfers between devices, passed_along(): return lax.ppermute(block, axis, route)  187 us
    all_gather x1, waiting for transfers between devices, ice_work(): lax.all_gather(adj_z, 'ice', axis=1, tiled=True)  58.8 us
    all_gather x1, waiting for transfers between devices, ice_work(): lax.all_gather(source, 'ice', axis=1, tiled=True)  58.4 us
  transfers between devices with their start and end apart: 69, of which 67 were waited for; matrix products, arithmetic and copies ran while one was open for 2% of the time, Pallas kernels for 0%

commit v1 on v0

v1 whole, which is shorter than its diff:
```python
import functools

import jax
import jax.numpy as jnp
from jax import lax
from jax.experimental import pallas as pl
from jax.experimental.pallas import tpu as pltpu
from jax.sharding import PartitionSpec as P

SUB = 8
WINDOWS = 2
COVERED = 32

PLASTIC = 0.25
VISCOUS = 1.0
GAMMA = 0.6
BETA = 0.9
STEP = 0.04

MESH = pl.DeviceIdType.MESH
FIELDS = 6
PHASES = ((0, 1), (1, 3), (3, 6))
GRADS = 4
BACK = ((0, 3), (3, 4))


def plan_kernel(work, covered, reinit, idx, keep, home, heavy):
    blocks = covered.shape[0]

    def clear(k, unused):
        idx[k] = 0
        keep[k] = 0
        return unused

    lax.fori_loop(0, idx.shape[0], clear, 0)

    def one(b, rank):
        place = jnp.minimum(rank, idx.shape[0] - 1)
        idx[place] = b
        keep[place] = 1 - reinit[b]
        home[b] = place
        return rank + covered[b]

    count = lax.fori_loop(0, blocks, one, 0)
    many = jnp.where(count > work, 1, 0)
    heavy[0] = many

    def fix(b, unused):
        home[b] = jnp.where(many == 1, home[b], work - 1)
        return unused

    lax.fori_loop(0, blocks, fix, 0)


def forward_diff(x, row, col):
    upper = jnp.where(row == 0, 0.0, pltpu.roll(x, 1, 0))
    left = jnp.where(col == 0, 0.0, pltpu.roll(x, 1, 1))
    return 2.0 * x - upper - left


def backward_diff(x, row, col):
    rows, cells = x.shape
    lower = jnp.where(row == rows - 1, 0.0, pltpu.roll(x, rows - 1, 0))
    right = jnp.where(col == cells - 1, 0.0, pltpu.roll(x, cells - 1, 1))
    return 2.0 * x - lower - right


def work_kernel(
    n, work, idx, keep, heavy, velo, stress, thick, force, switch, cot_u, cot_s, kernel, ret,
    own, over, got, keep_own, keep_over, keep_got, send, fields, zeta, total, grads,
    ex_send, ex_recv, go_send, go_recv, back_send, back_recv, fwd_send, fwd_recv,
):
    ocean = lax.axis_index("ocean")
    me = lax.axis_index("ice")
    other = 1 - ocean
    stride = n // work
    rows_dev = velo.shape[1]
    cells = velo.shape[2]
    rows = kernel.shape[0]
    my_slot = me // stride
    is_owner = me % stride == 0

    def when_owner(body):
        if stride == 1:
            body()
        else:
            pl.when(is_owner)(body)

    barrier = pltpu.get_barrier_semaphore()

    def greet(d, unused):
        pl.semaphore_signal(
            barrier, inc=1, device_id=(ocean, lax.rem(me + d, n)), device_id_type=MESH
        )
        return unused

    pl.semaphore_signal(barrier, inc=1, device_id=(other, me), device_id_type=MESH)
    lax.fori_loop(1, n, greet, 0)

    def pack(dst, keep_dst, k, rank):
        b = idx[rank]
        coef = jnp.where(switch[b] == 1, PLASTIC, VISCOUS)
        dst[0, k] = thick[b] * coef
        dst[1, k] = cot_u[b]
        dst[2, k] = cot_s[b]
        dst[3, k] = velo[b]
        dst[4, k] = stress[b]
        dst[5, k] = force[b]
        keep_dst[k] = jnp.full((rows_dev, cells), keep[rank].astype(jnp.float32))

    for k in range(work - 1):
        pack(over, keep_over, k, work + k)

    pl.semaphore_wait(barrier, n)

    def exchange(p):
        if p == len(PHASES):
            src, dst = keep_over, keep_got
        else:
            lo, hi = PHASES[p]
            src, dst = over.at[lo:hi], got.at[lo:hi]
        return pltpu.make_async_remote_copy(
            src_ref=src, dst_ref=dst, send_sem=ex_send.at[p], recv_sem=ex_recv.at[p],
            device_id=(other, me), device_id_type=MESH,
        )

    for p in range(len(PHASES) + 1):
        exchange(p).start()
    for k in range(work):
        pack(own, keep_own, k, k)

    full = jnp.full((rows_dev, cells), heavy[0]) == 1
    my_rows = pl.ds(pl.multiple_of(me * rows_dev, rows_dev), rows_dev)

    def go(p, slot, target):
        lo, hi = PHASES[p]
        return pltpu.make_async_remote_copy(
            src_ref=send.at[slot, lo:hi], dst_ref=fields.at[lo:hi, my_rows, :],
            send_sem=go_send.at[p, slot], recv_sem=go_recv.at[p, me],
            device_id=(ocean, target), device_id_type=MESH,
        )

    def arrive(p, j):
        lo, hi = PHASES[p]
        there = pl.ds(pl.multiple_of(j * rows_dev, rows_dev), rows_dev)
        return pltpu.make_async_remote_copy(
            src_ref=send.at[0, lo:hi], dst_ref=fields.at[lo:hi, there, :],
            send_sem=go_send.at[p, 0], recv_sem=go_recv.at[p, j],
            device_id=(ocean, j), device_id_type=MESH,
        )

    for p, (lo, hi) in enumerate(PHASES):
        exchange(p).wait_recv()
        for k in range(work):
            for f in range(lo, hi):
                rest = got[f, k] if k < work - 1 else own[f, 0]
                send[k, f] = jnp.where(full, own[f, k], rest)

        def start(d, unused, p=p):
            slot = lax.rem(my_slot + d, work)
            go(p, slot, slot * stride).start()
            return unused

        lax.fori_loop(1, work, start, 0)

        def local(lo=lo, hi=hi):
            fields[lo:hi, my_rows, :] = send[my_slot, lo:hi]

        when_owner(local)
        if stride > 1:
            pl.when(jnp.logical_not(is_owner))(lambda p=p: go(p, my_slot, my_slot * stride).start())
    exchange(len(PHASES)).wait_recv()

    def wait_phase(p):
        def one(d, unused):
            arrive(p, lax.rem(me + n - d, n)).wait_recv()
            return unused

        lax.fori_loop(1, n, one, 0)

    def back(p, j):
        lo, hi = BACK[p]
        there = pl.ds(pl.multiple_of(j * rows_dev, rows_dev), rows_dev)
        return pltpu.make_async_remote_copy(
            src_ref=grads.at[lo:hi, there, :], dst_ref=ret.at[lo:hi, my_slot],
            send_sem=back_send.at[p, j], recv_sem=back_recv.at[p, my_slot],
            device_id=(ocean, j), device_id_type=MESH,
        )

    def back_arrive(p, slot):
        lo, hi = BACK[p]
        return pltpu.make_async_remote_copy(
            src_ref=grads.at[lo:hi, my_rows, :], dst_ref=ret.at[lo:hi, slot],
            send_sem=back_send.at[p, 0], recv_sem=back_recv.at[p, slot],
            device_id=(ocean, slot * stride), device_id_type=MESH,
        )

    def send_back(p):
        lo, hi = BACK[p]

        def one(d, unused):
            back(p, lax.rem(me + d, n)).start()
            return unused

        lax.fori_loop(1, n, one, 0)
        ret[lo:hi, my_slot] = grads[lo:hi, my_rows, :]

    def compute():
        row = lax.broadcasted_iota(jnp.int32, (rows, cells), 0)
        col = lax.broadcasted_iota(jnp.int32, (rows, cells), 1)
        got_slot = jnp.minimum(my_slot, work - 2)
        spare = jnp.where(
            jnp.full((rows_dev, cells), my_slot) < work - 1, keep_got[got_slot], keep_own[0]
        )
        scale = jnp.where(full, keep_own[my_slot], spare)[:1]
        wait_phase(0)
        zeta[...] = jnp.dot(
            kernel[...], fields[0], precision=lax.Precision.HIGHEST,
            preferred_element_type=jnp.float32,
        )
        wait_phase(1)

        def retreat(step, carry, window):
            adj_u, adj_s, adj_f = carry
            total_s = adj_s - STEP * forward_diff(adj_u, row, col)
            total[window * SUB + SUB - 1 - step] = total_s
            adj_f = adj_f + STEP * adj_u
            adj_u = BETA * adj_u + backward_diff(zeta[...] * total_s, row, col)
            return adj_u, GAMMA * total_s, adj_f

        carry = (fields[1], fields[2], jnp.zeros((rows, cells), jnp.float32))
        for window in range(WINDOWS - 1, -1, -1):
            carry = lax.fori_loop(0, SUB, functools.partial(retreat, window=window), carry)
            if window > 0:
                carry = (carry[0], carry[1] * scale, carry[2])
        grads[0] = carry[0]
        grads[1] = carry[1]
        grads[2] = carry[2]
        send_back(0)
        wait_phase(2)

        def advance(step, carry, window):
            u_now, s_now, adj_z = carry
            strain = forward_diff(u_now, row, col)
            s_now = GAMMA * s_now + zeta[...] * strain
            u_now = BETA * u_now - STEP * backward_diff(s_now, row, col) + STEP * fields[5]
            adj_z = adj_z + total[window * SUB + step] * strain
            return u_now, s_now, adj_z

        carry = (fields[3], fields[4], jnp.zeros((rows, cells), jnp.float32))
        for window in range(WINDOWS):
            if window > 0:
                carry = (carry[0], carry[1] * scale, carry[2])
            carry = lax.fori_loop(0, SUB, functools.partial(advance, window=window), carry)
        grads[3] = lax.dot_general(
            kernel[...], carry[2], (((0,), (0,)), ((), ())),
            precision=lax.Precision.HIGHEST, preferred_element_type=jnp.float32,
        )
        send_back(1)

    when_owner(compute)

    def pass_on(p):
        lo, hi = BACK[p]
        return pltpu.make_async_remote_copy(
            src_ref=ret.at[lo:hi, 0 : work - 1], dst_ref=ret.at[lo:hi, work : 2 * work - 1],
            send_sem=fwd_send.at[p], recv_sem=fwd_recv.at[p],
            device_id=(other, me), device_id_type=MESH,
        )

    for p in range(len(BACK)):
        if stride > 1:
            pl.when(jnp.logical_not(is_owner))(lambda p=p: back_arrive(p, my_slot).wait_recv())

        def taken(d, unused, p=p):
            back_arrive(p, lax.rem(my_slot + d, work)).wait_recv()
            return unused

        lax.fori_loop(1, work, taken, 0)
        pass_on(p).start()

    for p in range(len(PHASES) + 1):
        exchange(p).wait_send()
    for p in range(len(PHASES)):

        def gone(d, unused, p=p):
            slot = lax.rem(my_slot + d, work)
            go(p, slot, slot * stride).wait_send()
            return unused

        lax.fori_loop(1, work, gone, 0)
        if stride > 1:
            pl.when(jnp.logical_not(is_owner))(
                lambda p=p: go(p, my_slot, my_slot * stride).wait_send()
            )

    def returned():
        for p in range(len(BACK)):

            def one(d, unused, p=p):
                back(p, lax.rem(me + d, n)).wait_send()
                return unused

            lax.fori_loop(1, n, one, 0)

    when_owner(returned)
    for p in range(len(BACK)):
        pass_on(p).wait()
    ret[:, 2 * work - 1] = jnp.zeros((GRADS, rows_dev, cells), jnp.float32)


def place_kernel(covered, home, ret, switch, grad_u, grad_s, grad_q, grad_f):
    blocks, rows_dev, cells = switch.shape

    def one(b, unused):
        slot = home[b]
        live = jnp.full((rows_dev, cells), covered[b]) == 1
        coef = jnp.where(switch[b] == 1, PLASTIC, VISCOUS)
        grad_u[b] = jnp.where(live, ret[0, slot], 0.0)
        grad_s[b] = jnp.where(live, ret[1, slot], 0.0)
        grad_f[b] = jnp.where(live, ret[2, slot], 0.0)
        grad_q[b] = jnp.where(live, ret[3, slot] * coef, 0.0)
        return unused

    lax.fori_loop(0, blocks, one, 0, unroll=8)


def shards(
    velocity, stress, thickness, forcing, switch, covered, reinit, cot_velocity, cot_stress, kernel
):
    blocks, rows_dev, cells = velocity.shape
    n = lax.axis_size("ice")
    work = COVERED // lax.axis_size("ocean")
    rows = kernel.shape[0]
    smem = pl.BlockSpec(memory_space=pltpu.SMEM)
    vmem = pl.BlockSpec(memory_space=pltpu.VMEM)
    i32, f32 = jnp.int32, jnp.float32
    tile = (rows_dev, cells)

    idx, keep, home, heavy = pl.pallas_call(
        functools.partial(plan_kernel, work),
        out_shape=[
            jax.ShapeDtypeStruct((2 * work,), i32),
            jax.ShapeDtypeStruct((2 * work,), i32),
            jax.ShapeDtypeStruct((blocks,), i32),
            jax.ShapeDtypeStruct((1,), i32),
        ],
        in_specs=[smem] * 2,
        out_specs=[smem] * 4,
    )(covered, reinit)

    ret = pl.pallas_call(
        functools.partial(work_kernel, n, work),
        out_shape=jax.ShapeDtypeStruct((GRADS, 2 * work) + tile, f32),
        in_specs=[smem] * 3 + [vmem] * 8,
        out_specs=vmem,
        scratch_shapes=[
            pltpu.VMEM((FIELDS, work) + tile, f32),
            pltpu.VMEM((FIELDS, work - 1) + tile, f32),
            pltpu.VMEM((FIELDS, work - 1) + tile, f32),
            pltpu.VMEM((work,) + tile, f32),
            pltpu.VMEM((work - 1,) + tile, f32),
            pltpu.VMEM((work - 1,) + tile, f32),
            pltpu.VMEM((work, FIELDS) + tile, f32),
            pltpu.VMEM((FIELDS, rows, cells), f32),
            pltpu.VMEM((rows, cells), f32),
            pltpu.VMEM((WINDOWS * SUB, rows, cells), f32),
            pltpu.VMEM((GRADS, rows, cells), f32),
            pltpu.SemaphoreType.DMA((len(PHASES) + 1,)),
            pltpu.SemaphoreType.DMA((len(PHASES) + 1,)),
            pltpu.SemaphoreType.DMA((len(PHASES), work)),
            pltpu.SemaphoreType.DMA((len(PHASES), n)),
            pltpu.SemaphoreType.DMA((len(BACK), n)),
            pltpu.SemaphoreType.DMA((len(BACK), work)),
            pltpu.SemaphoreType.DMA((len(BACK),)),
            pltpu.SemaphoreType.DMA((len(BACK),)),
        ],
        compiler_params=pltpu.CompilerParams(
            collective_id=0, has_side_effects=True, vmem_limit_bytes=40 << 20
        ),
    )(idx, keep, heavy, velocity, stress, thickness, forcing, switch, cot_velocity, cot_stress, kernel)

    field = jax.ShapeDtypeStruct(velocity.shape, f32)
    grad_u, grad_s, grad_q, grad_f = pl.pallas_call(
        place_kernel,
        out_shape=[field] * 4,
        in_specs=[smem] * 2 + [vmem] * 2,
        out_specs=[vmem] * 4,
    )(covered, home, ret, switch)
    return grad_u, grad_s, grad_q, grad_f


def solution(mesh):
    split = P("ocean", "ice", None)
    return jax.shard_map(
        shards,
        mesh=mesh,
        in_specs=(split,) * 5 + (P("ocean"),) * 2 + (split,) * 2 + (P(),),
        out_specs=(split,) * 4,
        check_vma=False,
    )
```

time: 593 us -> 44.9 us (0.08)
  waiting for transfers between devices: 306 us -> 0 us
  starting transfers between devices: 229 us -> 0 us
  Pallas kernels: 0 us -> 34.9 us
  other arithmetic: 16.6 us -> 0 us
  between operations: 14.4 us -> 0.68 us
  blocking collectives: 6.08 us -> 0 us
    ppermute x64 -> x0, starting transfers between devices: 219 us -> none  [passed_along(): return lax.ppermute(block, axis, route)]
    ppermute x64 -> x0, waiting for transfers between devices: 187 us -> none  [passed_along(): return lax.ppermute(block, axis, route)]
    all_gather x2 -> x0, waiting for transfers between devices: 117 us -> none  [the longest x1 58.8 us: ice_work(): lax.all_gather(adj_z, 'ice', axis=1, tiled=True)]
    pallas_call x0 -> x3, Pallas kernels: none -> 34.9 us  [the longest x1 30.2 us: shards(): pl.pallas_call(functools.partial(work_kernel, n, work), out_shape=jax.Sha...]
    all_to_all x3 -> x0, starting transfers between devices: 9.92 us -> none  [the longest x1 3.53 us: shards(): lax.all_to_all(packed, 'ocean', split_axis=0, concat_axis=0, tiled=True)]
  transfers between devices with their start and end apart: 69 -> 0, of which waited for: 67 -> 0; matrix products, arithmetic and copies ran while one was open for 2% -> 0% of each run, Pallas kernels for 0% -> 0%
where the time goes in v1:
time: 44.9 us; the launch traced here: 44.5 us
  Pallas kernels  34.9 us (78%)
  local copies, waits for them, and re-layouts  8.92 us (20%)
  between operations  0.68 us (2%)
    pallas_call x1, Pallas kernels, shards(): pl.pallas_call(functools.partial(work_kernel, n, work), out_shape=jax.Sha...  30.2 us
    unnamed x22, local copies, waits for them, and re-layouts  8.92 us
    pallas_call x1, Pallas kernels, shards(): pl.pallas_call(functools.partial(plan_kernel, work), out_shape=[jax.Shape...  2.44 us
    pallas_call x1, Pallas kernels, shards(): pl.pallas_call(place_kernel, out_shape=[field] * 4, in_specs=[smem] * 2 +...  2.27 us

profile of v1, /device:TPU:0, one launch (start us, length us, event | category | flops | bytes accessed | tf_op | source)
XLA Modules:
  0.0 44.5 jit_solution(14214264827497985567)
XLA Ops:
  0.6 2.4 %shard_map.129 = (s32[32]{0:T(128)}, s32[32]{0:T(128)}, s32[64]{0:T(128)}, s32[1]{0:T(128)}) custom-call(s32[64]{0:T(128)} %covered.3, s32[64]{0:T(128)} %reinit.1), custom_call_target="tpu_custom_call" | custom-call | tf_op jit(solution)/shard_map/pallas_call | solution.py:340
  3.1 0.0 copy-start.9
  3.1 0.0 copy-start.10
  3.1 0.6 %copy-done.9 = s32[32]{0:T(128)S(1)} copy-done((s32[32]{0:T(128)S(1)}, s32[32]{0:T(128)}, u32[]{:S(2)}) %copy-start.9) | copy-done | bytes 152
  3.7 0.0 copy-done.10
  3.8 0.0 copy-start.1
  3.8 0.9 %copy-done.1 = s32[64,8,128]{2,1,0:T(8,128)S(1)} copy-done((s32[64,8,128]{2,1,0:T(8,128)S(1)}, s32[64,8,128]{2,1,0:T(8,128)}, u32[]{:S(2)}) %copy-start.1) | copy-done | bytes 262168
  4.7 0.0 copy-start.2
  4.7 0.9 %copy-done.2 = f32[64,8,128]{2,1,0:T(8,128)S(1)} copy-done((f32[64,8,128]{2,1,0:T(8,128)S(1)}, f32[64,8,128]{2,1,0:T(8,128)}, u32[]{:S(2)}) %copy-start.2) | copy-done | bytes 262168
  5.7 0.0 copy-start.3
  5.7 0.9 %copy-done.3 = f32[64,8,128]{2,1,0:T(8,128)S(1)} copy-done((f32[64,8,128]{2,1,0:T(8,128)S(1)}, f32[64,8,128]{2,1,0:T(8,128)}, u32[]{:S(2)}) %copy-start.3) | copy-done | bytes 262168
  6.6 0.0 copy-start.4
  6.6 0.9 %copy-done.4 = f32[64,8,128]{2,1,0:T(8,128)S(1)} copy-done((f32[64,8,128]{2,1,0:T(8,128)S(1)}, f32[64,8,128]{2,1,0:T(8,128)}, u32[]{:S(2)}) %copy-start.4) | copy-done | bytes 262168
  7.6 0.0 copy-start.5
  7.6 0.9 %copy-done.5 = f32[64,8,128]{2,1,0:T(8,128)S(1)} copy-done((f32[64,8,128]{2,1,0:T(8,128)S(1)}, f32[64,8,128]{2,1,0:T(8,128)}, u32[]{:S(2)}) %copy-start.5) | copy-done | bytes 262168
  8.5 0.0 copy-start.6
  8.5 0.9 %copy-done.6 = f32[64,8,128]{2,1,0:T(8,128)S(1)} copy-done((f32[64,8,128]{2,1,0:T(8,128)S(1)}, f32[64,8,128]{2,1,0:T(8,128)}, u32[]{:S(2)}) %copy-start.6) | copy-done | bytes 262168
  9.5 0.0 copy-start.7
  9.5 0.9 %copy-done.7 = f32[64,8,128]{2,1,0:T(8,128)S(1)} copy-done((f32[64,8,128]{2,1,0:T(8,128)S(1)}, f32[64,8,128]{2,1,0:T(8,128)}, u32[]{:S(2)}) %copy-start.7) | copy-done | bytes 262168
  10.4 0.0 copy-start.8
  10.4 0.8 %copy-done.8 = f32[128,128]{1,0:T(8,128)S(1)} copy-done((f32[128,128]{1,0:T(8,128)S(1)}, f32[128,128]{1,0:T(8,128)}, u32[]{:S(2)}) %copy-start.8) | copy-done | bytes 65560
  11.2 30.2 %shard_map.130.ret = f32[4,32,8,128]{3,2,1,0:T(8,128)S(1)} custom-call(s32[32]{0:T(128)S(1)} %copy-done.9, s32[32]{0:T(128)S(1)} %copy-done.10, s32[1]{0:T(128)} %get-tuple-element.11.heavy, f32[64,8,128]{2,1,0:T(8,128)S(1)} %copy-done.2, f32[64,8,128]{2,1,0:T(8,128)S(1)} %copy-done.3, f32[64,8,128]{2,1,0:T(8,128)S(1)} %copy-done.4, ...), custom_call_target="tpu_custom_call" | custom-call | tf_op jit(solution)/shard_map/pallas_call | solution.py:352
  41.4 0.0 copy-start
  41.4 0.8 %copy-done = f32[4,32,8,128]{3,2,1,0:T(8,128)} copy-done((f32[4,32,8,128]{3,2,1,0:T(8,128)}, f32[4,32,8,128]{3,2,1,0:T(8,128)S(1)}, u32[]{:S(2)}) %copy-start) | copy-done | bytes 524312
  42.2 2.3 %shard_map.131 = (f32[64,8,128]{2,1,0:T(8,128)}, f32[64,8,128]{2,1,0:T(8,128)}, f32[64,8,128]{2,1,0:T(8,128)}, f32[64,8,128]{2,1,0:T(8,128)}) custom-call(s32[64]{0:T(128)} %covered.3, s32[64]{0:T(128)} %get-tuple-element.8.home, f32[4,32,8,128]{3,2,1,0:T(8,128)} %copy-done, s32[64,8,128]{2,1,0:T(8,128)} %switch.3), custom_call_target="tpu_custom_call" | custom-call | tf_op jit(solution)/shard_map/pallas_call | solution.py:384
Async XLA Ops:
  3.1 0.7 %copy-start.9 = (s32[32]{0:T(128)S(1)}, s32[32]{0:T(128)}, u32[]{:S(2)}) copy-start(s32[32]{0:T(128)} %get-tuple-element.9.idx) | copy-start | bytes 388
  3.1 0.7 %copy-start.10 = (s32[32]{0:T(128)S(1)}, s32[32]{0:T(128)}, u32[]{:S(2)}) copy-start(s32[32]{0:T(128)} %get-tuple-element.10.keep) | copy-start | bytes 388
  3.8 0.9 %copy-start.1 = (s32[64,8,128]{2,1,0:T(8,128)S(1)}, s32[64,8,128]{2,1,0:T(8,128)}, u32[]{:S(2)}) copy-start(s32[64,8,128]{2,1,0:T(8,128)} %switch.3) | copy-start | bytes 786436
  4.7 0.9 %copy-start.2 = (f32[64,8,128]{2,1,0:T(8,128)S(1)}, f32[64,8,128]{2,1,0:T(8,128)}, u32[]{:S(2)}) copy-start(f32[64,8,128]{2,1,0:T(8,128)} %velo.1) | copy-start | bytes 786436
  5.7 0.9 %copy-start.3 = (f32[64,8,128]{2,1,0:T(8,128)S(1)}, f32[64,8,128]{2,1,0:T(8,128)}, u32[]{:S(2)}) copy-start(f32[64,8,128]{2,1,0:T(8,128)} %stress.1) | copy-start | bytes 786436
  6.6 0.9 %copy-start.4 = (f32[64,8,128]{2,1,0:T(8,128)S(1)}, f32[64,8,128]{2,1,0:T(8,128)}, u32[]{:S(2)}) copy-start(f32[64,8,128]{2,1,0:T(8,128)} %thick.1) | copy-start | bytes 786436
  7.6 0.9 %copy-start.5 = (f32[64,8,128]{2,1,0:T(8,128)S(1)}, f32[64,8,128]{2,1,0:T(8,128)}, u32[]{:S(2)}) copy-start(f32[64,8,128]{2,1,0:T(8,128)} %force.1) | copy-start | bytes 786436
  8.5 0.9 %copy-start.6 = (f32[64,8,128]{2,1,0:T(8,128)S(1)}, f32[64,8,128]{2,1,0:T(8,128)}, u32[]{:S(2)}) copy-start(f32[64,8,128]{2,1,0:T(8,128)} %cot_u.1) | copy-start | bytes 786436
  9.5 0.9 %copy-start.7 = (f32[64,8,128]{2,1,0:T(8,128)S(1)}, f32[64,8,128]{2,1,0:T(8,128)}, u32[]{:S(2)}) copy-start(f32[64,8,128]{2,1,0:T(8,128)} %cot_s.1) | copy-start | bytes 786436
  10.4 0.8 %copy-start.8 = (f32[128,128]{1,0:T(8,128)S(1)}, f32[128,128]{1,0:T(8,128)}, u32[]{:S(2)}) copy-start(f32[128,128]{1,0:T(8,128)} %kernel.1) | copy-start | bytes 196612
  41.4 0.8 %copy-start = (f32[4,32,8,128]{3,2,1,0:T(8,128)}, f32[4,32,8,128]{3,2,1,0:T(8,128)S(1)}, u32[]{:S(2)}) copy-start(f32[4,32,8,128]{3,2,1,0:T(8,128)S(1)} %shard_map.130.ret) | copy-start | bytes 1572868

commit v2 on v1

--- a/solution.py
+++ b/solution.py
@@ -24,34 +24,6 @@
 BACK = ((0, 3), (3, 4))
 
 
-def plan_kernel(work, covered, reinit, idx, keep, home, heavy):
-    blocks = covered.shape[0]
-
-    def clear(k, unused):
-        idx[k] = 0
-        keep[k] = 0
-        return unused
-
-    lax.fori_loop(0, idx.shape[0], clear, 0)
-
-    def one(b, rank):
-        place = jnp.minimum(rank, idx.shape[0] - 1)
-        idx[place] = b
-        keep[place] = 1 - reinit[b]
-        home[b] = place
-        return rank + covered[b]
-
-    count = lax.fori_loop(0, blocks, one, 0)
-    many = jnp.where(count > work, 1, 0)
-    heavy[0] = many
-
-    def fix(b, unused):
-        home[b] = jnp.where(many == 1, home[b], work - 1)
-        return unused
-
-    lax.fori_loop(0, blocks, fix, 0)
-
-
 def forward_diff(x, row, col):
     upper = jnp.where(row == 0, 0.0, pltpu.roll(x, 1, 0))
     left = jnp.where(col == 0, 0.0, pltpu.roll(x, 1, 1))
@@ -66,10 +38,17 @@
 
 
 def work_kernel(
-    n, work, idx, keep, heavy, velo, stress, thick, force, switch, cot_u, cot_s, kernel, ret,
-    own, over, got, keep_own, keep_over, keep_got, send, fields, zeta, total, grads,
-    ex_send, ex_recv, go_send, go_recv, back_send, back_recv, fwd_send, fwd_recv,
+    n, work, covered_in, reinit_in, *refs
 ):
+    operands, ret, inputs, (covered, reinit, idx_row, idx), rest = (
+        refs[:8], refs[8], refs[9:17], refs[17:21], refs[21:]
+    )
+    velo, stress, thick, force, switch, cot_u, cot_s, kernel = inputs
+    (
+        own, over, got, keep_own, keep_over, keep_got, send, fields, zeta, total, grads,
+        in_sem, plan_sem, ex_send, ex_recv, go_send, go_recv, back_send, back_recv, own_sem,
+        fwd_send, fwd_recv,
+    ) = rest
     ocean = lax.axis_index("ocean")
     me = lax.axis_index("ice")
     other = 1 - ocean
@@ -86,6 +65,18 @@
         else:
             pl.when(is_owner)(body)
 
+    plan_in = (
+        pltpu.make_async_copy(covered_in, covered, plan_sem.at[0]),
+        pltpu.make_async_copy(reinit_in, reinit, plan_sem.at[1]),
+    )
+    fetch = [
+        pltpu.make_async_copy(operands[i], inputs[i], in_sem.at[i]) for i in range(len(operands))
+    ]
+    for copy in plan_in:
+        copy.start()
+    for i in (2, 4, 5, 6, 0, 1, 3, 7):
+        fetch[i].start()
+
     barrier = pltpu.get_barrier_semaphore()
 
     def greet(d, unused):
@@ -97,21 +88,39 @@
     pl.semaphore_signal(barrier, inc=1, device_id=(other, me), device_id_type=MESH)
     lax.fori_loop(1, n, greet, 0)
 
-    def pack(dst, keep_dst, k, rank):
-        b = idx[rank]
-        coef = jnp.where(switch[b] == 1, PLASTIC, VISCOUS)
-        dst[0, k] = thick[b] * coef
-        dst[1, k] = cot_u[b]
-        dst[2, k] = cot_s[b]
-        dst[3, k] = velo[b]
-        dst[4, k] = stress[b]
-        dst[5, k] = force[b]
-        keep_dst[k] = jnp.full((rows_dev, cells), keep[rank].astype(jnp.float32))
-
-    for k in range(work - 1):
-        pack(over, keep_over, k, work + k)
-
-    pl.semaphore_wait(barrier, n)
+    for copy in plan_in:
+        copy.wait()
+    blocks = covered.shape[1]
+    ones = jnp.broadcast_to(covered[...].astype(jnp.float32), (8, blocks))
+    upto = (
+        lax.broadcasted_iota(jnp.int32, (blocks, blocks), 1)
+        <= lax.broadcasted_iota(jnp.int32, (blocks, blocks), 0)
+    ).astype(jnp.float32)
+    tally = lax.dot_general(
+        upto, ones, (((1,), (1,)), ((), ())), preferred_element_type=jnp.float32
+    )
+    ranks = lax.broadcasted_iota(jnp.int32, (blocks, cells), 1).astype(jnp.float32)
+    before = jnp.where(jnp.broadcast_to(tally[:, :1], (blocks, cells)) <= ranks, 1, 0)
+    idx_row[...] = jnp.minimum(jnp.sum(before, axis=0, keepdims=True), blocks - 1)
+    to_scalars = pltpu.make_async_copy(idx_row, idx, plan_sem.at[2])
+    to_scalars.start()
+    count = jnp.sum(ones, axis=1, keepdims=True)[:1]
+    full = jnp.broadcast_to(count, (rows_dev, cells)) > work + 0.0
+
+    fetched = ((2, 4), (5, 6), (0, 1, 3))
+    sources = (None, cot_u, cot_s, velo, stress, force)
+
+    def pack(dst, k, rank, p):
+        b = idx[0, rank]
+        for f in range(*PHASES[p]):
+            if f == 0:
+                dst[f, k] = thick[b] * jnp.where(switch[b] == 1, PLASTIC, VISCOUS)
+            else:
+                dst[f, k] = sources[f][b]
+
+    def pack_keep(dst, k, rank):
+        kept = (1 - reinit[0, idx[0, rank]]).astype(jnp.float32)
+        dst[k] = jnp.full((rows_dev, cells), kept)
 
     def exchange(p):
         if p == len(PHASES):
@@ -124,12 +133,24 @@
             device_id=(other, me), device_id_type=MESH,
         )
 
-    for p in range(len(PHASES) + 1):
+    to_scalars.wait()
+    for p in range(len(PHASES)):
+        for i in fetched[p]:
+            fetch[i].wait()
+        for k in range(work - 1):
+            pack(over, k, work + k, p)
+        if p == 0:
+            pl.semaphore_wait(barrier, n)
         exchange(p).start()
+    for k in range(work - 1):
+        pack_keep(keep_over, k, work + k)
+    exchange(len(PHASES)).start()
+    for p in range(len(PHASES)):
+        for k in range(work):
+            pack(own, k, k, p)
     for k in range(work):
-        pack(own, keep_own, k, k)
-
-    full = jnp.full((rows_dev, cells), heavy[0]) == 1
+        pack_keep(keep_own, k, k)
+
     my_rows = pl.ds(pl.multiple_of(me * rows_dev, rows_dev), rows_dev)
 
     def go(p, slot, target):
@@ -187,6 +208,12 @@
             device_id=(ocean, j), device_id_type=MESH,
         )
 
+    def back_own(p):
+        lo, hi = BACK[p]
+        return pltpu.make_async_copy(
+            grads.at[lo:hi, my_rows, :], ret.at[lo:hi, my_slot], own_sem.at[p]
+        )
+
     def back_arrive(p, slot):
         lo, hi = BACK[p]
         return pltpu.make_async_remote_copy(
@@ -203,7 +230,7 @@
             return unused
 
         lax.fori_loop(1, n, one, 0)
-        ret[lo:hi, my_slot] = grads[lo:hi, my_rows, :]
+        back_own(p).start()
 
     def compute():
         row = lax.broadcasted_iota(jnp.int32, (rows, cells), 0)
@@ -213,6 +240,7 @@
             jnp.full((rows_dev, cells), my_slot) < work - 1, keep_got[got_slot], keep_own[0]
         )
         scale = jnp.where(full, keep_own[my_slot], spare)[:1]
+        fetch[7].wait()
         wait_phase(0)
         zeta[...] = jnp.dot(
             kernel[...], fields[0], precision=lax.Precision.HIGHEST,
@@ -259,6 +287,8 @@
         send_back(1)
 
     when_owner(compute)
+    if stride > 1:
+        pl.when(jnp.logical_not(is_owner))(lambda: fetch[7].wait())
 
     def pass_on(p):
         lo, hi = BACK[p]
@@ -277,6 +307,7 @@
             return unused
 
         lax.fori_loop(1, work, taken, 0)
+        when_owner(lambda p=p: back_own(p).wait())
         pass_on(p).start()
 
     for p in range(len(PHASES) + 1):
@@ -306,23 +337,41 @@
     when_owner(returned)
     for p in range(len(BACK)):
         pass_on(p).wait()
-    ret[:, 2 * work - 1] = jnp.zeros((GRADS, rows_dev, cells), jnp.float32)
-
-
-def place_kernel(covered, home, ret, switch, grad_u, grad_s, grad_q, grad_f):
+
+
+def place_kernel(work, covered_in, ret_in, switch_in, *refs):
+    outs, covered, ret, switch, placed, in_sem, out_sem = refs[:4], *refs[4:]
     blocks, rows_dev, cells = switch.shape
-
-    def one(b, unused):
-        slot = home[b]
-        live = jnp.full((rows_dev, cells), covered[b]) == 1
-        coef = jnp.where(switch[b] == 1, PLASTIC, VISCOUS)
-        grad_u[b] = jnp.where(live, ret[0, slot], 0.0)
-        grad_s[b] = jnp.where(live, ret[1, slot], 0.0)
-        grad_f[b] = jnp.where(live, ret[2, slot], 0.0)
-        grad_q[b] = jnp.where(live, ret[3, slot] * coef, 0.0)
-        return unused
-
-    lax.fori_loop(0, blocks, one, 0, unroll=8)
+    fetch = [
+        pltpu.make_async_copy(covered_in, covered, in_sem.at[0]),
+        pltpu.make_async_copy(switch_in, switch, in_sem.at[1]),
+    ] + [
+        pltpu.make_async_copy(ret_in.at[f], ret.at[f], in_sem.at[2 + f]) for f in range(GRADS)
+    ]
+    for copy in fetch:
+        copy.start()
+    fetch[0].wait()
+    rank = jnp.int32(0)
+    ranks = []
+    for b in range(blocks):
+        ranks.append(rank)
+        rank = rank + covered[0, b]
+    many = rank > work
+    homes = [
+        jnp.where(many, jnp.minimum(r, 2 * work - 2), work - 1) for r in ranks
+    ]
+    fetch[1].wait()
+    for f in range(GRADS):
+        fetch[2 + f].wait()
+        for b in range(blocks):
+            live = jnp.full((rows_dev, cells), covered[0, b]) == 1
+            value = ret[f, homes[b]]
+            if f == GRADS - 1:
+                value = value * jnp.where(switch[b] == 1, PLASTIC, VISCOUS)
+            placed[f, b] = jnp.where(live, value, 0.0)
+        pltpu.make_async_copy(placed.at[f], outs[f], out_sem.at[f]).start()
+    for f in range(GRADS):
+        pltpu.make_async_copy(placed.at[f], outs[f], out_sem.at[f]).wait()
 
 
 def shards(
@@ -332,29 +381,26 @@
     n = lax.axis_size("ice")
     work = COVERED // lax.axis_size("ocean")
     rows = kernel.shape[0]
-    smem = pl.BlockSpec(memory_space=pltpu.SMEM)
-    vmem = pl.BlockSpec(memory_space=pltpu.VMEM)
+    hbm = pl.BlockSpec(memory_space=pl.ANY)
     i32, f32 = jnp.int32, jnp.float32
     tile = (rows_dev, cells)
-
-    idx, keep, home, heavy = pl.pallas_call(
-        functools.partial(plan_kernel, work),
-        out_shape=[
-            jax.ShapeDtypeStruct((2 * work,), i32),
-            jax.ShapeDtypeStruct((2 * work,), i32),
-            jax.ShapeDtypeStruct((blocks,), i32),
-            jax.ShapeDtypeStruct((1,), i32),
-        ],
-        in_specs=[smem] * 2,
-        out_specs=[smem] * 4,
-    )(covered, reinit)
+    covered = covered.reshape(1, blocks)
+    reinit = reinit.reshape(1, blocks)
+    operands = (
+        velocity, stress, thickness, forcing, switch, cot_velocity, cot_stress, kernel
+    )
 
     ret = pl.pallas_call(
         functools.partial(work_kernel, n, work),
-        out_shape=jax.ShapeDtypeStruct((GRADS, 2 * work) + tile, f32),
-        in_specs=[smem] * 3 + [vmem] * 8,
-        out_specs=vmem,
-        scratch_shapes=[
+        out_shape=jax.ShapeDtypeStruct((GRADS, 2 * work - 1) + tile, f32),
+        in_specs=[hbm] * 10,
+        out_specs=hbm,
+        scratch_shapes=[pltpu.VMEM(x.shape, x.dtype) for x in operands]
+        + [
+            pltpu.VMEM((1, blocks), i32),
+            pltpu.SMEM((1, blocks), i32),
+            pltpu.VMEM((1, cells), i32),
+            pltpu.SMEM((1, cells), i32),
             pltpu.VMEM((FIELDS, work) + tile, f32),
             pltpu.VMEM((FIELDS, work - 1) + tile, f32),
             pltpu.VMEM((FIELDS, work - 1) + tile, f32),
@@ -366,6 +412,8 @@
             pltpu.VMEM((rows, cells), f32),
             pltpu.VMEM((WINDOWS * SUB, rows, cells), f32),
             pltpu.VMEM((GRADS, rows, cells), f32),
+            pltpu.SemaphoreType.DMA((len(operands),)),
+            pltpu.SemaphoreType.DMA((3,)),
             pltpu.SemaphoreType.DMA((len(PHASES) + 1,)),
             pltpu.SemaphoreType.DMA((len(PHASES) + 1,)),
             pltpu.SemaphoreType.DMA((len(PHASES), work)),
@@ -374,19 +422,29 @@
             pltpu.SemaphoreType.DMA((len(BACK), work)),
             pltpu.SemaphoreType.DMA((len(BACK),)),
             pltpu.SemaphoreType.DMA((len(BACK),)),
+            pltpu.SemaphoreType.DMA((len(BACK),)),
         ],
         compiler_params=pltpu.CompilerParams(
-            collective_id=0, has_side_effects=True, vmem_limit_bytes=40 << 20
+            collective_id=0, has_side_effects=True, vmem_limit_bytes=64 << 20
         ),
-    )(idx, keep, heavy, velocity, stress, thickness, forcing, switch, cot_velocity, cot_stress, kernel)
+    )(covered, reinit, *operands)
 
     field = jax.ShapeDtypeStruct(velocity.shape, f32)
-    grad_u, grad_s, grad_q, grad_f = pl.pallas_call(
-        place_kernel,
-        out_shape=[field] * 4,
-        in_specs=[smem] * 2 + [vmem] * 2,
-        out_specs=[vmem] * 4,
-    )(covered, home, ret, switch)
+    grad_u, grad_s, grad_f, grad_q = pl.pallas_call(
+        functools.partial(place_kernel, work),
+        out_shape=[field] * GRADS,
+        in_specs=[hbm] * 3,
+        out_specs=[hbm] * GRADS,
+        scratch_shapes=[
+            pltpu.SMEM((1, blocks), i32),
+            pltpu.VMEM(ret.shape, f32),
+            pltpu.VMEM(switch.shape, i32),
+            pltpu.VMEM((GRADS,) + velocity.shape, f32),
+            pltpu.SemaphoreType.DMA((2 + GRADS,)),
+            pltpu.SemaphoreType.DMA((GRADS,)),
+        ],
+        compiler_params=pltpu.CompilerParams(vmem_limit_bytes=64 << 20),
+    )(covered, ret, switch)
     return grad_u, grad_s, grad_q, grad_f
 
 

time: 44.9 us -> 32.4 us (0.72)
  local copies, waits for them, and re-layouts: 8.92 us -> 0 us
  Pallas kernels: 34.9 us -> 31.6 us
    unnamed x22 -> x0, local copies, waits for them, and re-layouts: 8.92 us -> none
    pallas_call x2 -> x1, Pallas kernels: 4.71 us -> 2.15 us  [shards(): pl.pallas_call(functools.partial(place_kernel, work), out_shape=[field] *...]
    pallas_call x1, Pallas kernels: 30.2 us -> 29.5 us  [shards(): pl.pallas_call(functools.partial(work_kernel, n, work), out_shape=jax.Sha...]
where the time goes in v2:
time: 32.4 us; the launch traced here: 32.3 us
  Pallas kernels  31.6 us (98%)
  between operations  0.64 us (2%)
    pallas_call x1, Pallas kernels, shards(): pl.pallas_call(functools.partial(work_kernel, n, work), out_shape=jax.Sha...  29.5 us
    pallas_call x1, Pallas kernels, shards(): pl.pallas_call(functools.partial(place_kernel, work), out_shape=[field] *...  2.15 us

profile of v2, /device:TPU:0, one launch (start us, length us, event | category | flops | bytes accessed | tf_op | source)
XLA Modules:
  0.0 32.3 jit_solution(1703958185834045407)
XLA Ops:
  0.6 29.5 %shard_map.129.ret_in = f32[4,31,8,128]{3,2,1,0:T(8,128)} custom-call(s32[1,64]{1,0:T(1,128)} %bitcast.2, s32[1,64]{1,0:T(1,128)} %bitcast.4, f32[64,8,128]{2,1,0:T(8,128)} %refs_0_.1, f32[64,8,128]{2,1,0:T(8,128)} %refs_1_.1, f32[64,8,128]{2,1,0:T(8,128)} %refs_2_.1, f32[64,8,128]{2,1,0:T(8,128)} %refs_3_.1, s32[64,8,128]{2,1,0:T(8,128)} %switch_in.1, ...), custom_call_target="tpu_custom_call" | custom-call | tf_op jit(solution)/shard_map/pallas_call | solution.py:393
  30.1 2.1 %shard_map.130 = (f32[64,8,128]{2,1,0:T(8,128)}, f32[64,8,128]{2,1,0:T(8,128)}, f32[64,8,128]{2,1,0:T(8,128)}, f32[64,8,128]{2,1,0:T(8,128)}) custom-call(s32[1,64]{1,0:T(1,128)} %bitcast.3, f32[4,31,8,128]{3,2,1,0:T(8,128)} %shard_map.129.ret_in, s32[64,8,128]{2,1,0:T(8,128)} %switch_in.1), custom_call_target="tpu_custom_call" | custom-call | tf_op jit(solution)/shard_map/pallas_call | solution.py:433

commit v3 on v2

--- a/solution.py
+++ b/solution.py
@@ -134,7 +134,8 @@
         )
 
     to_scalars.wait()
-    for p in range(len(PHASES)):
+
+    def pack_phase(p):
         for i in fetched[p]:
             fetch[i].wait()
         for k in range(work - 1):
@@ -142,14 +143,15 @@
         if p == 0:
             pl.semaphore_wait(barrier, n)
         exchange(p).start()
-    for k in range(work - 1):
-        pack_keep(keep_over, k, work + k)
-    exchange(len(PHASES)).start()
-    for p in range(len(PHASES)):
         for k in range(work):
             pack(own, k, k, p)
-    for k in range(work):
-        pack_keep(keep_own, k, k)
+
+    def pack_keeps():
+        for k in range(work - 1):
+            pack_keep(keep_over, k, work + k)
+        exchange(len(PHASES)).start()
+        for k in range(work):
+            pack_keep(keep_own, k, k)
 
     my_rows = pl.ds(pl.multiple_of(me * rows_dev, rows_dev), rows_dev)
 
@@ -170,6 +172,8 @@
             device_id=(ocean, j), device_id_type=MESH,
         )
 
+    pack_phase(0)
+    pack_phase(1)
     for p, (lo, hi) in enumerate(PHASES):
         exchange(p).wait_recv()
         for k in range(work):
@@ -190,6 +194,10 @@
         when_owner(local)
         if stride > 1:
             pl.when(jnp.logical_not(is_owner))(lambda p=p: go(p, my_slot, my_slot * stride).start())
+        if p == 0:
+            pack_phase(2)
+        elif p == 1:
+            pack_keeps()
     exchange(len(PHASES)).wait_recv()
 
     def wait_phase(p):
@@ -242,44 +250,45 @@
         scale = jnp.where(full, keep_own[my_slot], spare)[:1]
         fetch[7].wait()
         wait_phase(0)
-        zeta[...] = jnp.dot(
+        zeta[...] = -STEP * jnp.dot(
             kernel[...], fields[0], precision=lax.Precision.HIGHEST,
             preferred_element_type=jnp.float32,
         )
         wait_phase(1)
 
-        def retreat(step, carry, window):
-            adj_u, adj_s, adj_f = carry
-            total_s = adj_s - STEP * forward_diff(adj_u, row, col)
-            total[window * SUB + SUB - 1 - step] = total_s
-            adj_f = adj_f + STEP * adj_u
-            adj_u = BETA * adj_u + backward_diff(zeta[...] * total_s, row, col)
-            return adj_u, GAMMA * total_s, adj_f
-
-        carry = (fields[1], fields[2], jnp.zeros((rows, cells), jnp.float32))
-        for window in range(WINDOWS - 1, -1, -1):
-            carry = lax.fori_loop(0, SUB, functools.partial(retreat, window=window), carry)
-            if window > 0:
+        def retreat(carry, step):
+            adj, adj_s, adj_f = carry
+            total_s = adj_s + forward_diff(adj, row, col)
+            total[step] = total_s
+            adj_f = adj_f + adj
+            adj = BETA * adj + backward_diff(zeta[...] * total_s, row, col)
+            return adj, GAMMA * total_s, adj_f
+
+        carry = (-STEP * fields[1], fields[2], jnp.zeros((rows, cells), jnp.float32))
+        for step in range(WINDOWS * SUB - 1, -1, -1):
+            carry = retreat(carry, step)
+            if step > 0 and step % SUB == 0:
                 carry = (carry[0], carry[1] * scale, carry[2])
-        grads[0] = carry[0]
+        grads[0] = carry[0] * (-1.0 / STEP)
         grads[1] = carry[1]
-        grads[2] = carry[2]
+        grads[2] = -carry[2]
         send_back(0)
         wait_phase(2)
 
-        def advance(step, carry, window):
-            u_now, s_now, adj_z = carry
+        def advance(carry, step):
+            u_now, r_now, adj_z = carry
             strain = forward_diff(u_now, row, col)
-            s_now = GAMMA * s_now + zeta[...] * strain
-            u_now = BETA * u_now - STEP * backward_diff(s_now, row, col) + STEP * fields[5]
-            adj_z = adj_z + total[window * SUB + step] * strain
-            return u_now, s_now, adj_z
-
-        carry = (fields[3], fields[4], jnp.zeros((rows, cells), jnp.float32))
-        for window in range(WINDOWS):
-            if window > 0:
+            r_now = GAMMA * r_now + zeta[...] * strain
+            u_now = BETA * u_now + backward_diff(r_now, row, col) + fields[5]
+            adj_z = adj_z + total[step] * strain
+            return u_now, r_now, adj_z
+
+        fields[5] = STEP * fields[5]
+        carry = (fields[3], -STEP * fields[4], jnp.zeros((rows, cells), jnp.float32))
+        for step in range(WINDOWS * SUB):
+            if step > 0 and step % SUB == 0:
                 carry = (carry[0], carry[1] * scale, carry[2])
-            carry = lax.fori_loop(0, SUB, functools.partial(advance, window=window), carry)
+            carry = advance(carry, step)
         grads[3] = lax.dot_general(
             kernel[...], carry[2], (((0,), (0,)), ((), ())),
             precision=lax.Precision.HIGHEST, preferred_element_type=jnp.float32,

time: 32.4 us -> 31.8 us (0.981)
  Pallas kernels: 31.6 us -> 31 us
    pallas_call x1, Pallas kernels: 29.5 us -> 28.8 us  [shards(): pl.pallas_call(functools.partial(work_kernel, n, work), out_shape=jax.Sha...]
where the time goes in v3:
time: 31.8 us; the launch traced here: 31.6 us
  Pallas kernels  31 us (97%)
  between operations  0.64 us (2%)
    pallas_call x1, Pallas kernels, shards(): pl.pallas_call(functools.partial(work_kernel, n, work), out_shape=jax.Sha...  28.8 us
    pallas_call x1, Pallas kernels, shards(): pl.pallas_call(functools.partial(place_kernel, work), out_shape=[field] *...  2.15 us

profile of v3, /device:TPU:0, one launch (start us, length us, event | category | flops | bytes accessed | tf_op | source)
XLA Modules:
  0.0 31.6 jit_solution(2194985177370786107)
XLA Ops:
  0.6 28.8 %shard_map.129.ret_in = f32[4,31,8,128]{3,2,1,0:T(8,128)} custom-call(s32[1,64]{1,0:T(1,128)} %bitcast.2, s32[1,64]{1,0:T(1,128)} %bitcast.4, f32[64,8,128]{2,1,0:T(8,128)} %refs_0_.1, f32[64,8,128]{2,1,0:T(8,128)} %refs_1_.1, f32[64,8,128]{2,1,0:T(8,128)} %refs_2_.1, f32[64,8,128]{2,1,0:T(8,128)} %refs_3_.1, s32[64,8,128]{2,1,0:T(8,128)} %switch_in.1, ...), custom_call_target="tpu_custom_call" | custom-call | tf_op jit(solution)/shard_map/pallas_call | solution.py:402
  29.5 2.1 %shard_map.130 = (f32[64,8,128]{2,1,0:T(8,128)}, f32[64,8,128]{2,1,0:T(8,128)}, f32[64,8,128]{2,1,0:T(8,128)}, f32[64,8,128]{2,1,0:T(8,128)}) custom-call(s32[1,64]{1,0:T(1,128)} %bitcast.3, f32[4,31,8,128]{3,2,1,0:T(8,128)} %shard_map.129.ret_in, s32[64,8,128]{2,1,0:T(8,128)} %switch_in.1), custom_call_target="tpu_custom_call" | custom-call | tf_op jit(solution)/shard_map/pallas_call | solution.py:442

commit v4 on v3

--- a/solution.py
+++ b/solution.py
@@ -24,17 +24,42 @@
 BACK = ((0, 3), (3, 4))
 
 
-def forward_diff(x, row, col):
-    upper = jnp.where(row == 0, 0.0, pltpu.roll(x, 1, 0))
-    left = jnp.where(col == 0, 0.0, pltpu.roll(x, 1, 1))
-    return 2.0 * x - upper - left
-
-
-def backward_diff(x, row, col):
-    rows, cells = x.shape
-    lower = jnp.where(row == rows - 1, 0.0, pltpu.roll(x, rows - 1, 0))
-    right = jnp.where(col == cells - 1, 0.0, pltpu.roll(x, cells - 1, 1))
-    return 2.0 * x - lower - right
+SUBLANES = 8
+
+
+def load_tiles(ref, index, rows):
+    count = rows // SUBLANES
+    return [ref[index, pl.ds(v, SUBLANES, stride=count), :] for v in range(count)]
+
+
+def store_tiles(ref, index, tiles):
+    for v, tile in enumerate(tiles):
+        ref[index, pl.ds(v, SUBLANES, stride=len(tiles)), :] = tile
+
+
+def forward_diff(tiles, row, col):
+    first = jnp.where(row == 0, 0.0, pltpu.roll(tiles[-1], 1, 0))
+    out = []
+    for v, x in enumerate(tiles):
+        upper = tiles[v - 1] if v > 0 else first
+        left = jnp.where(col == 0, 0.0, pltpu.roll(x, 1, 1))
+        out.append((x + x - upper) - left)
+    return out
+
+
+def backward_diff(tiles, row, col):
+    last = jnp.where(row == SUBLANES - 1, 0.0, pltpu.roll(tiles[0], SUBLANES - 1, 0))
+    cells = tiles[0].shape[1]
+    out = []
+    for v, x in enumerate(tiles):
+        lower = tiles[v + 1] if v + 1 < len(tiles) else last
+        right = jnp.where(col == cells - 1, 0.0, pltpu.roll(x, cells - 1, 1))
+        out.append((x + x - lower) - right)
+    return out
+
+
+def far_first(d, n):
+    return n // 2 + (1 - 2 * (d % 2)) * ((d + 1) // 2)
 
 
 def work_kernel(
@@ -182,11 +207,11 @@
                 send[k, f] = jnp.where(full, own[f, k], rest)
 
         def start(d, unused, p=p):
-            slot = lax.rem(my_slot + d, work)
+            slot = lax.rem(my_slot + far_first(d, work), work)
             go(p, slot, slot * stride).start()
             return unused
 
-        lax.fori_loop(1, work, start, 0)
+        lax.fori_loop(0, work - 1, start, 0)
 
         def local(lo=lo, hi=hi):
             fields[lo:hi, my_rows, :] = send[my_slot, lo:hi]
@@ -234,63 +259,69 @@
         lo, hi = BACK[p]
 
         def one(d, unused):
-            back(p, lax.rem(me + d, n)).start()
+            back(p, lax.rem(me + far_first(d, n), n)).start()
             return unused
 
-        lax.fori_loop(1, n, one, 0)
+        lax.fori_loop(0, n - 1, one, 0)
         back_own(p).start()
 
     def compute():
-        row = lax.broadcasted_iota(jnp.int32, (rows, cells), 0)
-        col = lax.broadcasted_iota(jnp.int32, (rows, cells), 1)
+        row = lax.broadcasted_iota(jnp.int32, (SUBLANES, cells), 0)
+        col = lax.broadcasted_iota(jnp.int32, (SUBLANES, cells), 1)
         got_slot = jnp.minimum(my_slot, work - 2)
         spare = jnp.where(
             jnp.full((rows_dev, cells), my_slot) < work - 1, keep_got[got_slot], keep_own[0]
         )
         scale = jnp.where(full, keep_own[my_slot], spare)[:1]
+        scale = jnp.broadcast_to(scale, (SUBLANES, cells))
         fetch[7].wait()
         wait_phase(0)
-        zeta[...] = -STEP * jnp.dot(
+        zeta[0] = -STEP * jnp.dot(
             kernel[...], fields[0], precision=lax.Precision.HIGHEST,
             preferred_element_type=jnp.float32,
         )
         wait_phase(1)
-
-        def retreat(carry, step):
-            adj, adj_s, adj_f = carry
-            total_s = adj_s + forward_diff(adj, row, col)
-            total[step] = total_s
-            adj_f = adj_f + adj
-            adj = BETA * adj + backward_diff(zeta[...] * total_s, row, col)
-            return adj, GAMMA * total_s, adj_f
-
-        carry = (-STEP * fields[1], fields[2], jnp.zeros((rows, cells), jnp.float32))
+        tiles = range(rows // SUBLANES)
+        blank = jnp.zeros((SUBLANES, cells), jnp.float32)
+        scaled = load_tiles(zeta, 0, rows)
+
+        adj = [-STEP * x for x in load_tiles(fields, 1, rows)]
+        adj_s = load_tiles(fields, 2, rows)
+        adj_f = [blank for v in tiles]
         for step in range(WINDOWS * SUB - 1, -1, -1):
-            carry = retreat(carry, step)
+            diff = forward_diff(adj, row, col)
+            total_s = [adj_s[v] + diff[v] for v in tiles]
+            for v in tiles:
+                total[step, v] = total_s[v]
+            adj_f = [adj_f[v] + adj[v] for v in tiles]
+            diff = backward_diff([scaled[v] * total_s[v] for v in tiles], row, col)
+            adj = [BETA * adj[v] + diff[v] for v in tiles]
+            adj_s = [GAMMA * total_s[v] for v in tiles]
             if step > 0 and step % SUB == 0:
-                carry = (carry[0], carry[1] * scale, carry[2])
-        grads[0] = carry[0] * (-1.0 / STEP)
-        grads[1] = carry[1]
-        grads[2] = -carry[2]
+                adj_s = [x * scale for x in adj_s]
+        store_tiles(grads, 0, [x * (-1.0 / STEP) for x in adj])
+        store_tiles(grads, 1, adj_s)
+        store_tiles(grads, 2, [-x for x in adj_f])
         send_back(0)
         wait_phase(2)
 
-        def advance(carry, step):
-            u_now, r_now, adj_z = carry
-            strain = forward_diff(u_now, row, col)
-            r_now = GAMMA * r_now + zeta[...] * strain
-            u_now = BETA * u_now + backward_diff(r_now, row, col) + fields[5]
-            adj_z = adj_z + total[step] * strain
-            return u_now, r_now, adj_z
-
-        fields[5] = STEP * fields[5]
-        carry = (fields[3], -STEP * fields[4], jnp.zeros((rows, cells), jnp.float32))
+        u_now = load_tiles(fields, 3, rows)
+        r_now = [-STEP * x for x in load_tiles(fields, 4, rows)]
+        pushed = [STEP * x for x in load_tiles(fields, 5, rows)]
+        scaled = load_tiles(zeta, 0, rows)
+        adj_z = [blank for v in tiles]
         for step in range(WINDOWS * SUB):
             if step > 0 and step % SUB == 0:
-                carry = (carry[0], carry[1] * scale, carry[2])
-            carry = advance(carry, step)
+                r_now = [x * scale for x in r_now]
+            strain = forward_diff(u_now, row, col)
+            adj_z = [adj_z[v] + total[step, v] * strain[v] for v in tiles]
+            r_now = [GAMMA * r_now[v] + scaled[v] * strain[v] for v in tiles]
+            if step < WINDOWS * SUB - 1:
+                diff = backward_diff(r_now, row, col)
+                u_now = [BETA * u_now[v] + diff[v] + pushed[v] for v in tiles]
+        store_tiles(zeta, 1, adj_z)
         grads[3] = lax.dot_general(
-            kernel[...], carry[2], (((0,), (0,)), ((), ())),
+            kernel[...], zeta[1], (((0,), (0,)), ((), ())),
             precision=lax.Precision.HIGHEST, preferred_element_type=jnp.float32,
         )
         send_back(1)
@@ -418,8 +449,8 @@
             pltpu.VMEM((work - 1,) + tile, f32),
             pltpu.VMEM((work, FIELDS) + tile, f32),
             pltpu.VMEM((FIELDS, rows, cells), f32),
-            pltpu.VMEM((rows, cells), f32),
-            pltpu.VMEM((WINDOWS * SUB, rows, cells), f32),
+            pltpu.VMEM((2, rows, cells), f32),
+            pltpu.VMEM((WINDOWS * SUB, rows // SUBLANES, SUBLANES, cells), f32),
             pltpu.VMEM((GRADS, rows, cells), f32),
             pltpu.SemaphoreType.DMA((len(operands),)),
             pltpu.SemaphoreType.DMA((3,)),

time: 31.8 us -> 32.3 us (1.016)
  Pallas kernels: 31 us -> 31.5 us
    pallas_call x1, Pallas kernels: 28.8 us -> 29.3 us  [shards(): pl.pallas_call(functools.partial(work_kernel, n, work), out_shape=jax.Sha...]
where the time goes in v4:
time: 32.3 us; the launch traced here: 32.1 us
  Pallas kernels  31.5 us (98%)
  between operations  0.64 us (2%)
    pallas_call x1, Pallas kernels, shards(): pl.pallas_call(functools.partial(work_kernel, n, work), out_shape=jax.Sha...  29.3 us
    pallas_call x1, Pallas kernels, shards(): pl.pallas_call(functools.partial(place_kernel, work), out_shape=[field] *...  2.15 us

profile of v4, /device:TPU:0, one launch (start us, length us, event | category | flops | bytes accessed | tf_op | source)
XLA Modules:
  0.0 32.1 jit_solution(8530257855997928504)
XLA Ops:
  0.6 29.3 %shard_map.129.ret_in = f32[4,31,8,128]{3,2,1,0:T(8,128)} custom-call(s32[1,64]{1,0:T(1,128)} %bitcast.2, s32[1,64]{1,0:T(1,128)} %bitcast.4, f32[64,8,128]{2,1,0:T(8,128)} %refs_0_.1, f32[64,8,128]{2,1,0:T(8,128)} %refs_1_.1, f32[64,8,128]{2,1,0:T(8,128)} %refs_2_.1, f32[64,8,128]{2,1,0:T(8,128)} %refs_3_.1, s32[64,8,128]{2,1,0:T(8,128)} %switch_in.1, ...), custom_call_target="tpu_custom_call" | custom-call | tf_op jit(solution)/shard_map/pallas_call | solution.py:433
  30.0 2.1 %shard_map.130 = (f32[64,8,128]{2,1,0:T(8,128)}, f32[64,8,128]{2,1,0:T(8,128)}, f32[64,8,128]{2,1,0:T(8,128)}, f32[64,8,128]{2,1,0:T(8,128)}) custom-call(s32[1,64]{1,0:T(1,128)} %bitcast.3, f32[4,31,8,128]{3,2,1,0:T(8,128)} %shard_map.129.ret_in, s32[64,8,128]{2,1,0:T(8,128)} %switch_in.1), custom_call_target="tpu_custom_call" | custom-call | tf_op jit(solution)/shard_map/pallas_call | solution.py:473

commit v5 on v4

--- a/solution.py
+++ b/solution.py
@@ -58,8 +58,20 @@
     return out
 
 
-def far_first(d, n):
-    return n // 2 + (1 - 2 * (d % 2)) * ((d + 1) // 2)
+def flips(n):
+    far, near = list(range(n // 2, n)), list(range(1, n // 2))
+    near.sort(key=lambda x: (x & -x) * n - x, reverse=True)
+    return [x for pair in zip(far, near) for x in pair] + far[len(near):]
+
+
+def flipped(index, bits):
+    place = 1
+    moved = index
+    while place <= bits:
+        if bits & place:
+            moved = moved + place * (1 - 2 * ((index // place) % 2))
+        place *= 2
+    return moved
 
 
 def work_kernel(
@@ -70,7 +82,7 @@
     )
     velo, stress, thick, force, switch, cot_u, cot_s, kernel = inputs
     (
-        own, over, got, keep_own, keep_over, keep_got, send, fields, zeta, total, grads,
+        own, over, got, keep_own, keep_over, keep_got, send, arrived, fields, zeta, total, grads, outgoing,
         in_sem, plan_sem, ex_send, ex_recv, go_send, go_recv, back_send, back_recv, own_sem,
         fwd_send, fwd_recv,
     ) = rest
@@ -178,21 +190,19 @@
         for k in range(work):
             pack_keep(keep_own, k, k)
 
-    my_rows = pl.ds(pl.multiple_of(me * rows_dev, rows_dev), rows_dev)
 
     def go(p, slot, target):
         lo, hi = PHASES[p]
         return pltpu.make_async_remote_copy(
-            src_ref=send.at[slot, lo:hi], dst_ref=fields.at[lo:hi, my_rows, :],
+            src_ref=send.at[slot, lo:hi], dst_ref=arrived.at[me, lo:hi],
             send_sem=go_send.at[p, slot], recv_sem=go_recv.at[p, me],
             device_id=(ocean, target), device_id_type=MESH,
         )
 
     def arrive(p, j):
         lo, hi = PHASES[p]
-        there = pl.ds(pl.multiple_of(j * rows_dev, rows_dev), rows_dev)
         return pltpu.make_async_remote_copy(
-            src_ref=send.at[0, lo:hi], dst_ref=fields.at[lo:hi, there, :],
+            src_ref=send.at[0, lo:hi], dst_ref=arrived.at[j, lo:hi],
             send_sem=go_send.at[p, 0], recv_sem=go_recv.at[p, j],
             device_id=(ocean, j), device_id_type=MESH,
         )
@@ -206,15 +216,12 @@
                 rest = got[f, k] if k < work - 1 else own[f, 0]
                 send[k, f] = jnp.where(full, own[f, k], rest)
 
-        def start(d, unused, p=p):
-            slot = lax.rem(my_slot + far_first(d, work), work)
+        for bits in flips(work):
+            slot = flipped(my_slot, bits)
             go(p, slot, slot * stride).start()
-            return unused
-
-        lax.fori_loop(0, work - 1, start, 0)
 
         def local(lo=lo, hi=hi):
-            fields[lo:hi, my_rows, :] = send[my_slot, lo:hi]
+            arrived[me, lo:hi] = send[my_slot, lo:hi]
 
         when_owner(local)
         if stride > 1:
@@ -231,12 +238,14 @@
             return unused
 
         lax.fori_loop(1, n, one, 0)
+        for f in range(*PHASES[p]):
+            for j in range(n):
+                fields[f, j * rows_dev : (j + 1) * rows_dev, :] = arrived[j, f]
 
     def back(p, j):
         lo, hi = BACK[p]
-        there = pl.ds(pl.multiple_of(j * rows_dev, rows_dev), rows_dev)
         return pltpu.make_async_remote_copy(
-            src_ref=grads.at[lo:hi, there, :], dst_ref=ret.at[lo:hi, my_slot],
+            src_ref=outgoing.at[j, lo:hi], dst_ref=ret.at[my_slot, lo:hi],
             send_sem=back_send.at[p, j], recv_sem=back_recv.at[p, my_slot],
             device_id=(ocean, j), device_id_type=MESH,
         )
@@ -244,13 +253,13 @@
     def back_own(p):
         lo, hi = BACK[p]
         return pltpu.make_async_copy(
-            grads.at[lo:hi, my_rows, :], ret.at[lo:hi, my_slot], own_sem.at[p]
+            outgoing.at[me, lo:hi], ret.at[my_slot, lo:hi], own_sem.at[p]
         )
 
     def back_arrive(p, slot):
         lo, hi = BACK[p]
         return pltpu.make_async_remote_copy(
-            src_ref=grads.at[lo:hi, my_rows, :], dst_ref=ret.at[lo:hi, slot],
+            src_ref=outgoing.at[0, lo:hi], dst_ref=ret.at[slot, lo:hi],
             send_sem=back_send.at[p, 0], recv_sem=back_recv.at[p, slot],
             device_id=(ocean, slot * stride), device_id_type=MESH,
         )
@@ -258,11 +267,11 @@
     def send_back(p):
         lo, hi = BACK[p]
 
-        def one(d, unused):
-            back(p, lax.rem(me + far_first(d, n), n)).start()
-            return unused
-
-        lax.fori_loop(0, n - 1, one, 0)
+        for f in range(lo, hi):
+            for j in range(n):
+                outgoing[j, f] = grads[f, j * rows_dev : (j + 1) * rows_dev, :]
+        for bits in flips(n):
+            back(p, flipped(me, bits)).start()
         back_own(p).start()
 
     def compute():
@@ -333,7 +342,7 @@
     def pass_on(p):
         lo, hi = BACK[p]
         return pltpu.make_async_remote_copy(
-            src_ref=ret.at[lo:hi, 0 : work - 1], dst_ref=ret.at[lo:hi, work : 2 * work - 1],
+            src_ref=ret.at[0 : work - 1, lo:hi], dst_ref=ret.at[work : 2 * work - 1, lo:hi],
             send_sem=fwd_send.at[p], recv_sem=fwd_recv.at[p],
             device_id=(other, me), device_id_type=MESH,
         )
@@ -385,8 +394,7 @@
     fetch = [
         pltpu.make_async_copy(covered_in, covered, in_sem.at[0]),
         pltpu.make_async_copy(switch_in, switch, in_sem.at[1]),
-    ] + [
-        pltpu.make_async_copy(ret_in.at[f], ret.at[f], in_sem.at[2 + f]) for f in range(GRADS)
+        pltpu.make_async_copy(ret_in, ret, in_sem.at[2]),
     ]
     for copy in fetch:
         copy.start()
@@ -401,11 +409,11 @@
         jnp.where(many, jnp.minimum(r, 2 * work - 2), work - 1) for r in ranks
     ]
     fetch[1].wait()
+    fetch[2].wait()
     for f in range(GRADS):
-        fetch[2 + f].wait()
         for b in range(blocks):
             live = jnp.full((rows_dev, cells), covered[0, b]) == 1
-            value = ret[f, homes[b]]
+            value = ret[homes[b], f]
             if f == GRADS - 1:
                 value = value * jnp.where(switch[b] == 1, PLASTIC, VISCOUS)
             placed[f, b] = jnp.where(live, value, 0.0)
@@ -432,7 +440,7 @@
 
     ret = pl.pallas_call(
         functools.partial(work_kernel, n, work),
-        out_shape=jax.ShapeDtypeStruct((GRADS, 2 * work - 1) + tile, f32),
+        out_shape=jax.ShapeDtypeStruct((2 * work - 1, GRADS) + tile, f32),
         in_specs=[hbm] * 10,
         out_specs=hbm,
         scratch_shapes=[pltpu.VMEM(x.shape, x.dtype) for x in operands]
@@ -448,10 +456,12 @@
             pltpu.VMEM((work - 1,) + tile, f32),
             pltpu.VMEM((work - 1,) + tile, f32),
             pltpu.VMEM((work, FIELDS) + tile, f32),
+            pltpu.VMEM((n, FIELDS) + tile, f32),
             pltpu.VMEM((FIELDS, rows, cells), f32),
             pltpu.VMEM((2, rows, cells), f32),
             pltpu.VMEM((WINDOWS * SUB, rows // SUBLANES, SUBLANES, cells), f32),
             pltpu.VMEM((GRADS, rows, cells), f32),
+            pltpu.VMEM((n, GRADS) + tile, f32),
             pltpu.SemaphoreType.DMA((len(operands),)),
             pltpu.SemaphoreType.DMA((3,)),
             pltpu.SemaphoreType.DMA((len(PHASES) + 1,)),
@@ -480,7 +490,7 @@
             pltpu.VMEM(ret.shape, f32),
             pltpu.VMEM(switch.shape, i32),
             pltpu.VMEM((GRADS,) + velocity.shape, f32),
-            pltpu.SemaphoreType.DMA((2 + GRADS,)),
+            pltpu.SemaphoreType.DMA((3,)),
             pltpu.SemaphoreType.DMA((GRADS,)),
         ],
         compiler_params=pltpu.CompilerParams(vmem_limit_bytes=64 << 20),

time: 32.3 us -> 31.7 us (0.981)
  Pallas kernels: 31.5 us -> 30.9 us
    pallas_call x1, Pallas kernels: 29.3 us -> 28.7 us  [shards(): pl.pallas_call(functools.partial(work_kernel, n, work), out_shape=jax.Sha...]
where the time goes in v5:
time: 31.7 us; the launch traced here: 31.6 us
  Pallas kernels  30.9 us (97%)
  between operations  0.64 us (2%)
    pallas_call x1, Pallas kernels, shards(): pl.pallas_call(functools.partial(work_kernel, n, work), out_shape=jax.Sha...  28.7 us
    pallas_call x1, Pallas kernels, shards(): pl.pallas_call(functools.partial(place_kernel, work), out_shape=[field] *...  2.28 us

profile of v5, /device:TPU:0, one launch (start us, length us, event | category | flops | bytes accessed | tf_op | source)
XLA Modules:
  0.0 31.6 jit_solution(12282594602860166948)
XLA Ops:
  0.6 28.7 %shard_map.129.ret_in = f32[31,4,8,128]{3,2,1,0:T(8,128)} custom-call(s32[1,64]{1,0:T(1,128)} %bitcast.2, s32[1,64]{1,0:T(1,128)} %bitcast.4, f32[64,8,128]{2,1,0:T(8,128)} %refs_0_.1, f32[64,8,128]{2,1,0:T(8,128)} %refs_1_.1, f32[64,8,128]{2,1,0:T(8,128)} %refs_2_.1, f32[64,8,128]{2,1,0:T(8,128)} %refs_3_.1, s32[64,8,128]{2,1,0:T(8,128)} %switch_in.1, ...), custom_call_target="tpu_custom_call" | custom-call | tf_op jit(solution)/shard_map/pallas_call | solution.py:441
  29.3 2.3 %shard_map.130 = (f32[64,8,128]{2,1,0:T(8,128)}, f32[64,8,128]{2,1,0:T(8,128)}, f32[64,8,128]{2,1,0:T(8,128)}, f32[64,8,128]{2,1,0:T(8,128)}) custom-call(s32[1,64]{1,0:T(1,128)} %bitcast.3, f32[31,4,8,128]{3,2,1,0:T(8,128)} %shard_map.129.ret_in, s32[64,8,128]{2,1,0:T(8,128)} %switch_in.1), custom_call_target="tpu_custom_call" | custom-call | tf_op jit(solution)/shard_map/pallas_call | solution.py:483

commit v6 on v5

--- a/solution.py
+++ b/solution.py
@@ -22,6 +22,7 @@
 PHASES = ((0, 1), (1, 3), (3, 6))
 GRADS = 4
 BACK = ((0, 3), (3, 4))
+PARTS = 4
 
 
 SUBLANES = 8
@@ -82,7 +83,7 @@
     )
     velo, stress, thick, force, switch, cot_u, cot_s, kernel = inputs
     (
-        own, over, got, keep_own, keep_over, keep_got, send, arrived, fields, zeta, total, grads, outgoing,
+        own, over, got, keep_own, keep_over, keep_got, send, arrived, fields, zeta, total, grads, outgoing, landed,
         in_sem, plan_sem, ex_send, ex_recv, go_send, go_recv, back_send, back_recv, own_sem,
         fwd_send, fwd_recv,
     ) = rest
@@ -245,21 +246,21 @@
     def back(p, j):
         lo, hi = BACK[p]
         return pltpu.make_async_remote_copy(
-            src_ref=outgoing.at[j, lo:hi], dst_ref=ret.at[my_slot, lo:hi],
+            src_ref=outgoing.at[j, lo:hi], dst_ref=landed.at[my_slot, lo:hi],
             send_sem=back_send.at[p, j], recv_sem=back_recv.at[p, my_slot],
             device_id=(ocean, j), device_id_type=MESH,
         )
 
-    def back_own(p):
+    def keep_own_part(p):
         lo, hi = BACK[p]
         return pltpu.make_async_copy(
-            outgoing.at[me, lo:hi], ret.at[my_slot, lo:hi], own_sem.at[p]
+            landed.at[:, lo:hi], ret.at[0:work, lo:hi], own_sem.at[p]
         )
 
     def back_arrive(p, slot):
         lo, hi = BACK[p]
         return pltpu.make_async_remote_copy(
-            src_ref=outgoing.at[0, lo:hi], dst_ref=ret.at[slot, lo:hi],
+            src_ref=outgoing.at[0, lo:hi], dst_ref=landed.at[slot, lo:hi],
             send_sem=back_send.at[p, 0], recv_sem=back_recv.at[p, slot],
             device_id=(ocean, slot * stride), device_id_type=MESH,
         )
@@ -272,7 +273,7 @@
                 outgoing[j, f] = grads[f, j * rows_dev : (j + 1) * rows_dev, :]
         for bits in flips(n):
             back(p, flipped(me, bits)).start()
-        back_own(p).start()
+        landed[my_slot, lo:hi] = outgoing[me, lo:hi]
 
     def compute():
         row = lax.broadcasted_iota(jnp.int32, (SUBLANES, cells), 0)
@@ -342,7 +343,7 @@
     def pass_on(p):
         lo, hi = BACK[p]
         return pltpu.make_async_remote_copy(
-            src_ref=ret.at[0 : work - 1, lo:hi], dst_ref=ret.at[work : 2 * work - 1, lo:hi],
+            src_ref=landed.at[0 : work - 1, lo:hi], dst_ref=ret.at[work : 2 * work - 1, lo:hi],
             send_sem=fwd_send.at[p], recv_sem=fwd_recv.at[p],
             device_id=(other, me), device_id_type=MESH,
         )
@@ -356,8 +357,8 @@
             return unused
 
         lax.fori_loop(1, work, taken, 0)
-        when_owner(lambda p=p: back_own(p).wait())
         pass_on(p).start()
+        keep_own_part(p).start()
 
     for p in range(len(PHASES) + 1):
         exchange(p).wait_send()
@@ -386,6 +387,7 @@
     when_owner(returned)
     for p in range(len(BACK)):
         pass_on(p).wait()
+        keep_own_part(p).wait()
 
 
 def place_kernel(work, covered_in, ret_in, switch_in, *refs):
@@ -410,16 +412,26 @@
     ]
     fetch[1].wait()
     fetch[2].wait()
-    for f in range(GRADS):
-        for b in range(blocks):
-            live = jnp.full((rows_dev, cells), covered[0, b]) == 1
-            value = ret[homes[b], f]
+    part = blocks // PARTS
+    sent = []
+    for b in range(blocks):
+        live = jnp.full((rows_dev, cells), covered[0, b]) == 1
+        home = homes[b]
+        for f in range(GRADS):
+            value = ret[home, f]
             if f == GRADS - 1:
                 value = value * jnp.where(switch[b] == 1, PLASTIC, VISCOUS)
             placed[f, b] = jnp.where(live, value, 0.0)
-        pltpu.make_async_copy(placed.at[f], outs[f], out_sem.at[f]).start()
-    for f in range(GRADS):
-        pltpu.make_async_copy(placed.at[f], outs[f], out_sem.at[f]).wait()
+        if (b + 1) % part == 0:
+            for f in range(GRADS):
+                span = pl.ds(b + 1 - part, part)
+                copy = pltpu.make_async_copy(
+                    placed.at[f, span], outs[f].at[span], out_sem.at[f, b // part]
+                )
+                copy.start()
+                sent.append(copy)
+    for copy in sent:
+        copy.wait()
 
 
 def shards(
@@ -462,6 +474,7 @@
             pltpu.VMEM((WINDOWS * SUB, rows // SUBLANES, SUBLANES, cells), f32),
             pltpu.VMEM((GRADS, rows, cells), f32),
             pltpu.VMEM((n, GRADS) + tile, f32),
+            pltpu.VMEM((work, GRADS) + tile, f32),
             pltpu.SemaphoreType.DMA((len(operands),)),
             pltpu.SemaphoreType.DMA((3,)),
             pltpu.SemaphoreType.DMA((len(PHASES) + 1,)),
@@ -491,7 +504,7 @@
             pltpu.VMEM(switch.shape, i32),
             pltpu.VMEM((GRADS,) + velocity.shape, f32),
             pltpu.SemaphoreType.DMA((3,)),
-            pltpu.SemaphoreType.DMA((GRADS,)),
+            pltpu.SemaphoreType.DMA((GRADS, PARTS)),
         ],
         compiler_params=pltpu.CompilerParams(vmem_limit_bytes=64 << 20),
     )(covered, ret, switch)

time: 31.7 us -> 31.4 us (level)
  no operation moved by 1% of the time
where the time goes in v6:
time: 31.4 us; the launch traced here: 31.3 us
  Pallas kernels  30.6 us (97%)
  between operations  0.64 us (2%)
    pallas_call x1, Pallas kernels, shards(): pl.pallas_call(functools.partial(work_kernel, n, work), out_shape=jax.Sha...  28.4 us
    pallas_call x1, Pallas kernels, shards(): pl.pallas_call(functools.partial(place_kernel, work), out_shape=[field] *...  2.27 us

profile of v6, /device:TPU:0, one launch (start us, length us, event | category | flops | bytes accessed | tf_op | source)
XLA Modules:
  0.0 31.3 jit_solution(16936642866092466617)
XLA Ops:
  0.6 28.4 %shard_map.129.ret_in = f32[31,4,8,128]{3,2,1,0:T(8,128)} custom-call(s32[1,64]{1,0:T(1,128)} %bitcast.2, s32[1,64]{1,0:T(1,128)} %bitcast.4, f32[64,8,128]{2,1,0:T(8,128)} %refs_0_.1, f32[64,8,128]{2,1,0:T(8,128)} %refs_1_.1, f32[64,8,128]{2,1,0:T(8,128)} %refs_2_.1, f32[64,8,128]{2,1,0:T(8,128)} %refs_3_.1, s32[64,8,128]{2,1,0:T(8,128)} %switch_in.1, ...), custom_call_target="tpu_custom_call" | custom-call | tf_op jit(solution)/shard_map/pallas_call | solution.py:453
  29.0 2.3 %shard_map.130 = (f32[64,8,128]{2,1,0:T(8,128)}, f32[64,8,128]{2,1,0:T(8,128)}, f32[64,8,128]{2,1,0:T(8,128)}, f32[64,8,128]{2,1,0:T(8,128)}) custom-call(s32[1,64]{1,0:T(1,128)} %bitcast.3, f32[31,4,8,128]{3,2,1,0:T(8,128)} %shard_map.129.ret_in, s32[64,8,128]{2,1,0:T(8,128)} %switch_in.1), custom_call_target="tpu_custom_call" | custom-call | tf_op jit(solution)/shard_map/pallas_call | solution.py:496
